TPU v7x, 256 devices: a whole 4x4x8 slice. The times are simulated.
256 devices in a mesh: gx: 8 (over x, y_hi), gy: 4 (over y_lo, core), gz: 8 (over z).
Axes of the slice: x: 4, y: 4 (y_hi: 2, y_lo: 2; y = y_hi * 2 + y_lo), z: 8, core: 2. Of those that a mesh axis runs over, the one named last changes fastest.
Arguments:
- seed_cotangent: bfloat16 [8, 4, 8, 112, 2048], P('gx', 'gy', 'gz'), may hold values from -6 to 6
- trace_operator: bfloat16 [8, 4, 8, 2048, 2048], P('gx', 'gy', 'gz'), may hold values from -0.125 to 0.125
- face_matrices: bfloat16 [8, 4, 8, 6, 340, 340], P('gx', 'gy', 'gz'), may hold values from -0.3125 to 0.3125
- saved_traces: bfloat16 [8, 4, 8, 3, 112, 2048], P('gx', 'gy', 'gz'), may hold values from -6 to 6
- edge_flags: int32 [8, 4, 8, 6], P('gx', 'gy', 'gz'), may hold values 0 or 1
- node_map: int32 [8, 4, 8, 6, 340], P('gx', 'gy', 'gz'), may hold values from 0 to 339, each once within a row
Outputs:
- adjoint_traces: bfloat16 [8, 4, 8, 112, 2048], P('gx', 'gy', 'gz')
- face_gradient: bfloat16 [8, 4, 8, 6, 340, 340], P('gx', 'gy', 'gz')
Inputs may be any that keep to these rules, and one draw needn't show every extreme that they name: Each row node_map[.., k, :] names every face node once.
All inputs are finite; a program needn't handle non-finite values. No bound on the sum of `edge_flags` on one device may be relied on, other than what follows from the above.
Results may differ from a plain program's by a relative error of at most 0.0085.
Values may be sent and summed in bfloat16 or wider, within the bound.
No kernel may reach another device: no remote copies, remote signals or barrier semaphores. Data moves between devices by JAX's collectives and lax.ppermute only.
A program may use at most 64 MiB of HBM per device.

v0:
```python
import math

import jax
import jax.numpy as jnp
from jax import lax
from jax.sharding import PartitionSpec as P


def with_halo(cells, sides, width):
    for axis, dim in sides:
        count = lax.axis_size(axis)
        ends = count - 1
        head = lax.slice_in_dim(cells, 0, width, axis=dim)
        tail = lax.slice_in_dim(cells, cells.shape[dim] - width, cells.shape[dim], axis=dim)
        cells = jnp.concatenate(
            [
                lax.ppermute(tail, axis, [(i, (i + 1) % count) for i in range(ends)]),
                cells,
                lax.ppermute(head, axis, [((i + 1) % count, i) for i in range(ends)]),
            ],
            axis=dim,
        )
    return cells


def face_block(array, number, width):
    return array[:, number * width : (number + 1) * width]


def axis_faces(block, width, axis_number):
    paired = jnp.stack([block[:, :width], block[:, width : 2 * width]], axis=0)
    if axis_number == 0:
        padded = with_halo(paired, (("gx", 0),), 1)
    elif axis_number == 1:
        padded = with_halo(paired, (("gy", 0),), 1)
    else:
        padded = with_halo(paired, (("gz", 0),), 1)
    return [padded[0], padded[3]]


def local(seed_cotangent, trace_operator, face_matrices, saved_traces, edge_flags, node_map):
    seeded = seed_cotangent[0, 0, 0].astype(jnp.float32)
    operator = trace_operator[0, 0, 0]
    matrices = face_matrices[0, 0, 0]
    stored = saved_traces[0, 0, 0]
    flagged = edge_flags[0, 0, 0]
    mapping = node_map[0, 0, 0]
    width = matrices.shape[-1]
    span = 6 * width
    sweeps = stored.shape[0]
    columns = seeded.shape[0]
    edge_mask = flagged[:, None, None] == 1
    node_ids = lax.broadcasted_iota(jnp.int32, (6, width, width), 1)
    selector = (mapping[:, None, :] == node_ids).astype(jnp.float32)
    placed = jnp.einsum(
        "kij,kjg->kig", selector.astype(jnp.bfloat16), matrices, preferred_element_type=jnp.float32
    ).astype(jnp.bfloat16)
    weights_used = jnp.where(edge_mask, matrices, placed)
    state = seeded
    gradient = jnp.zeros(matrices.shape, jnp.float32)
    for sweep in range(sweeps):
        lowered = state.astype(jnp.bfloat16)
        pieces = []
        hidden = jnp.dot(lowered, operator, preferred_element_type=jnp.float32).astype(jnp.bfloat16)
        for axis_number in range(3):
            block = hidden[:, 2 * axis_number * width : (2 * axis_number + 2) * width]
            pieces = pieces + axis_faces(block, width, axis_number)
        received = jnp.stack(pieces, axis=0)
        own = jnp.stack([face_block(hidden, number, width) for number in range(6)], axis=0)
        inputs = jnp.where(edge_mask, own, received)
        fresh = jnp.einsum("kcf,kfg->kcg", inputs, weights_used, preferred_element_type=jnp.float32)
        state = (
            jnp.concatenate(
                [fresh[number] for number in range(6)] + [hidden[:, span:].astype(jnp.float32)],
                axis=1,
            )
            + seeded
        )
        earlier = stored[sweeps - 1 - sweep]
        stored_faces = jnp.stack(
            [face_block(earlier, number, width) for number in range(6)], axis=0
        )
        gradient = gradient + jnp.einsum(
            "kcf,kcg->kfg", inputs, stored_faces, preferred_element_type=jnp.float32
        )
    permuted = jnp.einsum(
        "kij,kig->kjg",
        selector,
        gradient,
        precision=lax.Precision.HIGHEST,
        preferred_element_type=jnp.float32,
    )
    gradient = jnp.where(edge_mask, gradient, permuted)
    adjoint_traces = state.astype(jnp.bfloat16)
    face_gradient = (gradient * (1.0 / math.sqrt(columns))).astype(jnp.bfloat16)
    return (adjoint_traces[None, None, None], face_gradient[None, None, None])


def solution(mesh):
    return jax.shard_map(
        local,
        mesh=mesh,
        in_specs=(
            P("gx", "gy", "gz", None, None),
            P("gx", "gy", "gz", None, None),
            P("gx", "gy", "gz", None, None, None),
            P("gx", "gy", "gz", None, None, None),
            P("gx", "gy", "gz", None),
            P("gx", "gy", "gz", None, None),
        ),
        out_specs=(P("gx", "gy", "gz", None, None), P("gx", "gy", "gz", None, None, None)),
        check_vma=False,
    )
```

profile of v0, /device:TPU:120, one launch (start us, length us, event | category | flops | bytes accessed | tf_op | source)
XLA Modules:
  0.0 123.8 jit_solution(13120052628498444611)
XLA Ops:
  0.7 5.0 %fusion.7 = bf16[112,2048]{1,0:T(8,128)(2,1)S(1)} fusion(bf16[1,1,1,2048,2048]{4,3,2,1,0:T(8,128)(2,1)} %param.7, bf16[1,1,1,112,2048]{4,3,2,1,0:T(8,128)(2,1)} %param.6), kind=kOutput, calls=%fused_computation.11 | convolution fusion | flops 939753472 | bytes 9306112 | tf_op jit(solution)/shard_map/dot_general | solution.py:64
  5.6 0.2 slice_bitcast_fusion.52
  5.9 2.0 %collective-permute-start.5 = (bf16[1,112,340]{2,1,0:T(8,128)(2,1)S(1)}, bf16[1,112,340]{2,1,0:T(8,128)(2,1)S(1)}, u32[]{:S(2)}, u32[]{:S(2)}) collective-permute-start(bf16[1,112,340]{2,1,0:T(8,128)(2,1)S(1)} %get-tuple-element.35), channel_id=1, source_target_pairs={{1,0},{2,1},{3,2},{4,3},{5,4},{6,5},{7,6},{9,8},{10,9},{11,10},{12... | collective-permute-start | bytes 228488 | tf_op jit(solution)/shard_map/ppermute | solution.py:19
  7.9 5.0 %collective-permute-start.4 = (bf16[1,112,340]{2,1,0:T(8,128)(2,1)S(1)}, bf16[1,112,340]{2,1,0:T(8,128)(2,1)S(1)}, u32[]{:S(2)}, u32[]{:S(2)}) collective-permute-start(bf16[1,112,340]{2,1,0:T(8,128)(2,1)S(1)} %get-tuple-element.36), channel_id=1, source_target_pairs={{0,1},{1,2},{2,3},{3,4},{4,5},{5,6},{6,7},{8,9},{9,10},{10,11},{11... | collective-permute-start | bytes 228488 | tf_op jit(solution)/shard_map/ppermute | solution.py:17
  12.9 1.9 %collective-permute-start.2 = (bf16[1,112,340]{2,1,0:T(8,128)(2,1)S(1)}, bf16[1,112,340]{2,1,0:T(8,128)(2,1)S(1)}, u32[]{:S(2)}, u32[]{:S(2)}) collective-permute-start(bf16[1,112,340]{2,1,0:T(8,128)(2,1)S(1)} %get-tuple-element.37), channel_id=1, source_target_pairs={{0,8},{8,16},{16,24},{1,9},{9,17},{17,25},{2,10},{10,18},{18,26},{... | collective-permute-start | bytes 228488 | tf_op jit(solution)/shard_map/ppermute | solution.py:17
  14.9 3.6 %collective-permute-start.3 = (bf16[1,112,340]{2,1,0:T(8,128)(2,1)S(1)}, bf16[1,112,340]{2,1,0:T(8,128)(2,1)S(1)}, u32[]{:S(2)}, u32[]{:S(2)}) collective-permute-start(bf16[1,112,340]{2,1,0:T(8,128)(2,1)S(1)} %get-tuple-element.38), channel_id=1, source_target_pairs={{8,0},{16,8},{24,16},{9,1},{17,9},{25,17},{10,2},{18,10},{26,18},{... | collective-permute-start | bytes 228488 | tf_op jit(solution)/shard_map/ppermute | solution.py:19
  18.5 4.0 %collective-permute-start = (bf16[1,112,340]{2,1,0:T(8,128)(2,1)S(1)}, bf16[1,112,340]{2,1,0:T(8,128)(2,1)S(1)}, u32[]{:S(2)}, u32[]{:S(2)}) collective-permute-start(bf16[1,112,340]{2,1,0:T(8,128)(2,1)S(1)} %get-tuple-element.39), channel_id=1, source_target_pairs={{0,32},{32,64},{64,96},{96,128},{128,160},{160,192},{192,224},{1,3... | collective-permute-start | bytes 228488 | tf_op jit(solution)/shard_map/ppermute | solution.py:17
  22.7 0.1 constant_dynamic-update-slice_fusion.3
  22.9 0.1 constant_dynamic-update-slice_fusion.1
  23.0 0.1 constant_dynamic-update-slice_fusion
  23.3 0.1 constant_dynamic-update-slice_fusion.46
  23.4 0.1 constant_dynamic-update-slice_fusion.45
  23.5 0.1 constant_dynamic-update-slice_fusion.44
  23.6 0.1 constant_dynamic-update-slice_fusion.43
  23.8 0.1 constant_dynamic-update-slice_fusion.39
  23.9 0.1 constant_dynamic-update-slice_fusion.38
  24.0 0.1 constant_dynamic-update-slice_fusion.37
  24.2 0.1 constant_dynamic-update-slice_fusion.51
  24.3 0.1 constant_dynamic-update-slice_fusion.50
  24.5 0.1 constant_dynamic-update-slice_fusion.49
  24.7 0.1 constant_dynamic-update-slice_fusion.36
  24.8 0.6 copy-done.14
  25.5 0.8 copy-done.10
  26.2 0.8 copy-done.12
  27.1 2.3 %fusion.16 = bf16[6,340,340]{2,1,0:T(8,128)(2,1)S(1)} fusion(bf16[1,1,1,6,340,340]{5,4,3,2,1,0:T(8,128)(2,1)S(1)} %copy-done.17, s32[6,340]{1,0:T(8,128)S(1)} %bitcast.239, pred[6]{0:T(512)(128)(4,1)S(1)} %compare_bitcast_fusion), kind=kOutput, calls=%fused_computation.15 | convolution fusion | flops 475116000 | bytes 2782566 | tf_op jit(solution)/shard_map/kij,kjg->kig/dot_general | solution.py:55
  29.4 3.4 %collective-permute-start.1 = (bf16[1,112,340]{2,1,0:T(8,128)(2,1)S(1)}, bf16[1,112,340]{2,1,0:T(8,128)(2,1)S(1)}, u32[]{:S(2)}, u32[]{:S(2)}) collective-permute-start(bf16[1,112,340]{2,1,0:T(8,128)(2,1)S(1)} %get-tuple-element.40), channel_id=1, source_target_pairs={{32,0},{64,32},{96,64},{128,96},{160,128},{192,160},{224,192},{33,... | collective-permute-start | bytes 228488 | tf_op jit(solution)/shard_map/ppermute | solution.py:19
  32.8 5.4 %collective-permute-done.1 = bf16[1,112,340]{2,1,0:T(8,128)(2,1)S(1)} collective-permute-done((bf16[1,112,340]{2,1,0:T(8,128)(2,1)S(1)}, bf16[1,112,340]{2,1,0:T(8,128)(2,1)S(1)}, u32[]{:S(2)}, u32[]{:S(2)}) %collective-permute-start.1) | collective-permute-done | bytes 76192 | tf_op jit(solution)/shard_map/ppermute | solution.py:19
  38.4 0.6 fusion.33
  39.0 0.8 slice_bitcast_fusion.15
  39.8 1.5 %concatenate.68 = f32[1,1,1,112,2048]{4,3,2,1,0:T(8,128)S(1)} concatenate(f32[1,1,1,112,340]{4,3,2,1,0:T(8,128)} %get-tuple-element.22, f32[1,1,1,112,340]{4,3,2,1,0:T(8,128)} %get-tuple-element.21, f32[1,1,1,112,340]{4,3,2,1,0:T(8,128)} %get-tuple-element.20, f32[1,1,1,112,340]{4,3,2,1,0:T(8,128)S(1)} %get-tuple-element.19, f32[1,1,1,112,340]{4,3,2,1,0:T(8,128)S(1)} %get-tuple-element.18, ...), dimensions={4} | concatenate | bytes 1835008 | tf_op jit(solution)/shard_map/concatenate | solution.py:73
  41.3 4.9 %fusion.10 = bf16[112,2048]{1,0:T(8,128)(2,1)S(1)} fusion(bf16[1,1,1,2048,2048]{4,3,2,1,0:T(8,128)(2,1)} %param.7, f32[1,1,1,112,2048]{4,3,2,1,0:T(8,128)S(1)} %concatenate.68, bf16[1,1,1,112,2048]{4,3,2,1,0:T(8,128)(2,1)S(1)} %copy-done), kind=kOutput, calls=%fused_computation.12 | convolution fusion | flops 940441600 | bytes 10223616 | tf_op jit(solution)/shard_map/dot_general | solution.py:64
  46.2 0.2 slice_bitcast_fusion.46
  46.9 0.1 constant_dynamic-update-slice_fusion.12
  47.0 3.3 %collective-permute-start.6 = (bf16[1,112,340]{2,1,0:T(8,128)(2,1)S(1)}, bf16[1,112,340]{2,1,0:T(8,128)(2,1)S(1)}, u32[]{:S(2)}, u32[]{:S(2)}) collective-permute-start(bf16[1,112,340]{2,1,0:T(8,128)(2,1)S(1)} %get-tuple-element.33), channel_id=1, source_target_pairs={{0,32},{32,64},{64,96},{96,128},{128,160},{160,192},{192,224},{1,3... | collective-permute-start | bytes 228488 | tf_op jit(solution)/shard_map/ppermute | solution.py:17
  50.4 2.8 %fusion.32 = f32[6,340,340]{2,1,0:T(8,128)} fusion(bf16[6,112,340]{2,1,0:T(8,128)(2,1)S(1)} %copy-done.13, bf16[6,112,340]{2,1,0:T(8,128)(2,1)S(1)} %copy-done.8, bf16[6,112,340]{2,1,0:T(8,128)(2,1)S(1)} %copy-done.4, pred[6]{0:T(512)(128)(4,1)S(1)} %compare_bitcast_fusion), kind=kOutput, calls=%fused_computation.151 | convolution fusion | flops 155594880 | bytes 4145286 | tf_op jit(solution)/shard_map/kcf,kcg->kfg/dot_general | solution.py:83
  53.2 1.9 %collective-permute-start.11 = (bf16[1,112,340]{2,1,0:T(8,128)(2,1)S(1)}, bf16[1,112,340]{2,1,0:T(8,128)(2,1)S(1)}, u32[]{:S(2)}, u32[]{:S(2)}) collective-permute-start(bf16[1,112,340]{2,1,0:T(8,128)(2,1)S(1)} %get-tuple-element.29), channel_id=1, source_target_pairs={{1,0},{2,1},{3,2},{4,3},{5,4},{6,5},{7,6},{9,8},{10,9},{11,10},{12... | collective-permute-start | bytes 228488 | tf_op jit(solution)/shard_map/ppermute | solution.py:19
  55.2 5.1 %collective-permute-start.10 = (bf16[1,112,340]{2,1,0:T(8,128)(2,1)S(1)}, bf16[1,112,340]{2,1,0:T(8,128)(2,1)S(1)}, u32[]{:S(2)}, u32[]{:S(2)}) collective-permute-start(bf16[1,112,340]{2,1,0:T(8,128)(2,1)S(1)} %get-tuple-element.30), channel_id=1, source_target_pairs={{0,1},{1,2},{2,3},{3,4},{4,5},{5,6},{6,7},{8,9},{9,10},{10,11},{11... | collective-permute-start | bytes 228488 | tf_op jit(solution)/shard_map/ppermute | solution.py:17
  60.3 1.9 %collective-permute-start.8 = (bf16[1,112,340]{2,1,0:T(8,128)(2,1)S(1)}, bf16[1,112,340]{2,1,0:T(8,128)(2,1)S(1)}, u32[]{:S(2)}, u32[]{:S(2)}) collective-permute-start(bf16[1,112,340]{2,1,0:T(8,128)(2,1)S(1)} %get-tuple-element.31), channel_id=1, source_target_pairs={{0,8},{8,16},{16,24},{1,9},{9,17},{17,25},{2,10},{10,18},{18,26},{... | collective-permute-start | bytes 228488 | tf_op jit(solution)/shard_map/ppermute | solution.py:17
  62.2 3.6 %collective-permute-start.9 = (bf16[1,112,340]{2,1,0:T(8,128)(2,1)S(1)}, bf16[1,112,340]{2,1,0:T(8,128)(2,1)S(1)}, u32[]{:S(2)}, u32[]{:S(2)}) collective-permute-start(bf16[1,112,340]{2,1,0:T(8,128)(2,1)S(1)} %get-tuple-element.32), channel_id=1, source_target_pairs={{8,0},{16,8},{24,16},{9,1},{17,9},{25,17},{10,2},{18,10},{26,18},{... | collective-permute-start | bytes 228488 | tf_op jit(solution)/shard_map/ppermute | solution.py:19
  65.9 4.0 %collective-permute-start.7 = (bf16[1,112,340]{2,1,0:T(8,128)(2,1)S(1)}, bf16[1,112,340]{2,1,0:T(8,128)(2,1)S(1)}, u32[]{:S(2)}, u32[]{:S(2)}) collective-permute-start(bf16[1,112,340]{2,1,0:T(8,128)(2,1)S(1)} %get-tuple-element.34), channel_id=1, source_target_pairs={{32,0},{64,32},{96,64},{128,96},{160,128},{192,160},{224,192},{33,... | collective-permute-start | bytes 228488 | tf_op jit(solution)/shard_map/ppermute | solution.py:19
  69.9 4.8 %collective-permute-done.7 = bf16[1,112,340]{2,1,0:T(8,128)(2,1)S(1)} collective-permute-done((bf16[1,112,340]{2,1,0:T(8,128)(2,1)S(1)}, bf16[1,112,340]{2,1,0:T(8,128)(2,1)S(1)}, u32[]{:S(2)}, u32[]{:S(2)}) %collective-permute-start.7) | collective-permute-done | bytes 76192 | tf_op jit(solution)/shard_map/ppermute | solution.py:19
  74.8 0.6 fusion.35
  75.5 1.0 slice_bitcast_fusion.9
  76.5 1.7 %concatenate.77 = f32[1,1,1,112,2048]{4,3,2,1,0:T(8,128)S(1)} concatenate(f32[1,1,1,112,340]{4,3,2,1,0:T(8,128)} %get-tuple-element.16, f32[1,1,1,112,340]{4,3,2,1,0:T(8,128)} %get-tuple-element.15, f32[1,1,1,112,340]{4,3,2,1,0:T(8,128)} %get-tuple-element.14, f32[1,1,1,112,340]{4,3,2,1,0:T(8,128)} %get-tuple-element.13, f32[1,1,1,112,340]{4,3,2,1,0:T(8,128)} %get-tuple-element.12, ...), dimensions={4} | concatenate | bytes 1835008 | tf_op jit(solution)/shard_map/concatenate | solution.py:73
  78.2 4.8 %fusion.13 = bf16[112,2048]{1,0:T(8,128)(2,1)S(1)} fusion(bf16[1,1,1,2048,2048]{4,3,2,1,0:T(8,128)(2,1)} %param.7, f32[1,1,1,112,2048]{4,3,2,1,0:T(8,128)S(1)} %concatenate.77, bf16[1,1,1,112,2048]{4,3,2,1,0:T(8,128)(2,1)S(1)} %copy-done), kind=kOutput, calls=%fused_computation.13 | convolution fusion | flops 940441600 | bytes 10223616 | tf_op jit(solution)/shard_map/dot_general | solution.py:64
  83.1 0.2 slice_bitcast_fusion.40
  83.4 0.1 constant_dynamic-update-slice_fusion.27
  83.5 0.1 constant_dynamic-update-slice_fusion.26
  83.6 0.1 constant_dynamic-update-slice_fusion.25
  83.8 4.1 %collective-permute-start.12 = (bf16[1,112,340]{2,1,0:T(8,128)(2,1)S(1)}, bf16[1,112,340]{2,1,0:T(8,128)(2,1)S(1)}, u32[]{:S(2)}, u32[]{:S(2)}) collective-permute-start(bf16[1,112,340]{2,1,0:T(8,128)(2,1)S(1)} %get-tuple-element.27), channel_id=1, source_target_pairs={{0,32},{32,64},{64,96},{96,128},{128,160},{160,192},{192,224},{1,3... | collective-permute-start | bytes 228488 | tf_op jit(solution)/shard_map/ppermute | solution.py:17
  88.0 2.8 %fusion.34 = f32[6,340,340]{2,1,0:T(8,128)} fusion(bf16[6,112,340]{2,1,0:T(8,128)(2,1)S(1)} %copy-done.11, bf16[6,112,340]{2,1,0:T(8,128)(2,1)S(1)} %constant_dynamic-update-slice_fusion.12, bf16[6,112,340]{2,1,0:T(8,128)(2,1)S(1)} %copy-done.6, pred[6]{0:T(512)(128)(4,1)S(1)} %compare_bitcast_fusion), kind=kOutput, calls=%fused_computation.153 | convolution fusion | flops 155594880 | bytes 4145286 | tf_op jit(solution)/shard_map/kcf,kcg->kfg/dot_general | solution.py:83
  90.8 1.9 %collective-permute-start.17 = (bf16[1,112,340]{2,1,0:T(8,128)(2,1)S(1)}, bf16[1,112,340]{2,1,0:T(8,128)(2,1)S(1)}, u32[]{:S(2)}, u32[]{:S(2)}) collective-permute-start(bf16[1,112,340]{2,1,0:T(8,128)(2,1)S(1)} %get-tuple-element.23), channel_id=1, source_target_pairs={{1,0},{2,1},{3,2},{4,3},{5,4},{6,5},{7,6},{9,8},{10,9},{11,10},{12... | collective-permute-start | bytes 228488 | tf_op jit(solution)/shard_map/ppermute | solution.py:19
  92.8 5.1 %collective-permute-start.16 = (bf16[1,112,340]{2,1,0:T(8,128)(2,1)S(1)}, bf16[1,112,340]{2,1,0:T(8,128)(2,1)S(1)}, u32[]{:S(2)}, u32[]{:S(2)}) collective-permute-start(bf16[1,112,340]{2,1,0:T(8,128)(2,1)S(1)} %get-tuple-element.24), channel_id=1, source_target_pairs={{0,1},{1,2},{2,3},{3,4},{4,5},{5,6},{6,7},{8,9},{9,10},{10,11},{11... | collective-permute-start | bytes 228488 | tf_op jit(solution)/shard_map/ppermute | solution.py:17
  97.9 1.9 %collective-permute-start.14 = (bf16[1,112,340]{2,1,0:T(8,128)(2,1)S(1)}, bf16[1,112,340]{2,1,0:T(8,128)(2,1)S(1)}, u32[]{:S(2)}, u32[]{:S(2)}) collective-permute-start(bf16[1,112,340]{2,1,0:T(8,128)(2,1)S(1)} %get-tuple-element.25), channel_id=1, source_target_pairs={{0,8},{8,16},{16,24},{1,9},{9,17},{17,25},{2,10},{10,18},{18,26},{... | collective-permute-start | bytes 228488 | tf_op jit(solution)/shard_map/ppermute | solution.py:17
  99.8 3.6 %collective-permute-start.15 = (bf16[1,112,340]{2,1,0:T(8,128)(2,1)S(1)}, bf16[1,112,340]{2,1,0:T(8,128)(2,1)S(1)}, u32[]{:S(2)}, u32[]{:S(2)}) collective-permute-start(bf16[1,112,340]{2,1,0:T(8,128)(2,1)S(1)} %get-tuple-element.26), channel_id=1, source_target_pairs={{8,0},{16,8},{24,16},{9,1},{17,9},{25,17},{10,2},{18,10},{26,18},{... | collective-permute-start | bytes 228488 | tf_op jit(solution)/shard_map/ppermute | solution.py:19
  103.5 3.4 %collective-permute-start.13 = (bf16[1,112,340]{2,1,0:T(8,128)(2,1)S(1)}, bf16[1,112,340]{2,1,0:T(8,128)(2,1)S(1)}, u32[]{:S(2)}, u32[]{:S(2)}) collective-permute-start(bf16[1,112,340]{2,1,0:T(8,128)(2,1)S(1)} %get-tuple-element.28), channel_id=1, source_target_pairs={{32,0},{64,32},{96,64},{128,96},{160,128},{192,160},{224,192},{33,... | collective-permute-start | bytes 228488 | tf_op jit(solution)/shard_map/ppermute | solution.py:19
  106.9 5.3 %collective-permute-done.13 = bf16[1,112,340]{2,1,0:T(8,128)(2,1)S(1)} collective-permute-done((bf16[1,112,340]{2,1,0:T(8,128)(2,1)S(1)}, bf16[1,112,340]{2,1,0:T(8,128)(2,1)S(1)}, u32[]{:S(2)}, u32[]{:S(2)}) %collective-permute-start.13) | collective-permute-done | bytes 76192 | tf_op jit(solution)/shard_map/ppermute | solution.py:19
  112.4 0.6 fusion.37
  113.1 0.8 slice_bitcast_fusion.3
  113.9 1.6 %concatenate.86 = f32[1,1,1,112,2048]{4,3,2,1,0:T(8,128)S(1)} concatenate(f32[1,1,1,112,340]{4,3,2,1,0:T(8,128)} %get-tuple-element.10, f32[1,1,1,112,340]{4,3,2,1,0:T(8,128)} %get-tuple-element.9, f32[1,1,1,112,340]{4,3,2,1,0:T(8,128)} %get-tuple-element.8, f32[1,1,1,112,340]{4,3,2,1,0:T(8,128)} %get-tuple-element.7, f32[1,1,1,112,340]{4,3,2,1,0:T(8,128)S(1)} %get-tuple-element.6, ...), dimensions={4} | concatenate | bytes 1835008 | tf_op jit(solution)/shard_map/concatenate | solution.py:73
  115.5 0.9 fusion.23
  116.4 1.1 fusion.36
  117.5 1.0 copy-done.2
  118.5 5.3 %fusion.20 = bf16[1,1,1,6,340,340]{5,4,3,2,1,0:T(8,128)(2,1)} fusion(f32[6,340,340]{2,1,0:T(8,128)S(1)} %fusion.36, f32[6,340,340]{2,1,0:T(8,128)S(1)} %copy-done.1, f32[6,340,340]{2,1,0:T(8,128)S(1)} %copy-done.2, s32[6,340]{1,0:T(8,128)S(1)} %bitcast.240, pred[6]{0:T(512)(128)(4,1)S(1)} %compare_bitcast_fusion), kind=kOutput, calls=%fused_computation.19 | convolution fusion | flops 2835436800 | bytes 9718566 | tf_op jit(solution)/shard_map/kij,kig->kjg/dot_general | solution.py:86
  (90 shorter events, 2.0 us)
Async XLA Ops:
  0.6 21.9 %copy-start.18 = (s32[1,1,1,6]{3,2,1,0:T(1,128)S(1)}, s32[1,1,1,6]{3,2,1,0:T(1,128)}, u32[]{:S(2)}) copy-start(s32[1,1,1,6]{3,2,1,0:T(1,128)} %param.10) | copy-start | bytes 76
  0.6 21.9 %copy-start.16 = (s32[1,1,1,6,340]{4,2,3,1,0:T(1,128)S(1)}, s32[1,1,1,6,340]{4,2,3,1,0:T(1,128)}, u32[]{:S(2)}) copy-start(s32[1,1,1,6,340]{4,2,3,1,0:T(1,128)} %param.11) | copy-start | bytes 24484
  0.7 22.5 %copy-start.9 = (bf16[1,1,1,3,112,2048]{5,4,3,2,1,0:T(8,128)(2,1)S(1)}, bf16[1,1,1,3,112,2048]{5,4,3,2,1,0:T(8,128)(2,1)}, u32[]{:S(2)}) copy-start(bf16[1,1,1,3,112,2048]{5,4,3,2,1,0:T(8,128)(2,1)} %param.9) | copy-start | bytes 4128772
  5.9 32.5 %collective-permute-start.5 = (bf16[1,112,340]{2,1,0:T(8,128)(2,1)S(1)}, bf16[1,112,340]{2,1,0:T(8,128)(2,1)S(1)}, u32[]{:S(2)}, u32[]{:S(2)}) collective-permute-start(bf16[1,112,340]{2,1,0:T(8,128)(2,1)S(1)} %get-tuple-element.35), channel_id=1, source_target_pairs={{1,0},{2,1},{3,2},{4,3},{5,4},{6,5},{7,6},{9,8},{10,9},{11,10},{12... | collective-permute-start | bytes 228488 | tf_op jit(solution)/shard_map/ppermute | solution.py:19
  7.9 30.4 %collective-permute-start.4 = (bf16[1,112,340]{2,1,0:T(8,128)(2,1)S(1)}, bf16[1,112,340]{2,1,0:T(8,128)(2,1)S(1)}, u32[]{:S(2)}, u32[]{:S(2)}) collective-permute-start(bf16[1,112,340]{2,1,0:T(8,128)(2,1)S(1)} %get-tuple-element.36), channel_id=1, source_target_pairs={{0,1},{1,2},{2,3},{3,4},{4,5},{5,6},{6,7},{8,9},{9,10},{10,11},{11... | collective-permute-start | bytes 228488 | tf_op jit(solution)/shard_map/ppermute | solution.py:17
  12.9 25.3 %collective-permute-start.2 = (bf16[1,112,340]{2,1,0:T(8,128)(2,1)S(1)}, bf16[1,112,340]{2,1,0:T(8,128)(2,1)S(1)}, u32[]{:S(2)}, u32[]{:S(2)}) collective-permute-start(bf16[1,112,340]{2,1,0:T(8,128)(2,1)S(1)} %get-tuple-element.37), channel_id=1, source_target_pairs={{0,8},{8,16},{16,24},{1,9},{9,17},{17,25},{2,10},{10,18},{18,26},{... | collective-permute-start | bytes 228488 | tf_op jit(solution)/shard_map/ppermute | solution.py:17
  14.9 23.4 %collective-permute-start.3 = (bf16[1,112,340]{2,1,0:T(8,128)(2,1)S(1)}, bf16[1,112,340]{2,1,0:T(8,128)(2,1)S(1)}, u32[]{:S(2)}, u32[]{:S(2)}) collective-permute-start(bf16[1,112,340]{2,1,0:T(8,128)(2,1)S(1)} %get-tuple-element.38), channel_id=1, source_target_pairs={{8,0},{16,8},{24,16},{9,1},{17,9},{25,17},{10,2},{18,10},{26,18},{... | collective-permute-start | bytes 228488 | tf_op jit(solution)/shard_map/ppermute | solution.py:19
  18.5 10.9 %collective-permute-start = (bf16[1,112,340]{2,1,0:T(8,128)(2,1)S(1)}, bf16[1,112,340]{2,1,0:T(8,128)(2,1)S(1)}, u32[]{:S(2)}, u32[]{:S(2)}) collective-permute-start(bf16[1,112,340]{2,1,0:T(8,128)(2,1)S(1)} %get-tuple-element.39), channel_id=1, source_target_pairs={{0,32},{32,64},{64,96},{96,128},{128,160},{160,192},{192,224},{1,3... | collective-permute-start | bytes 228488 | tf_op jit(solution)/shard_map/ppermute | solution.py:17
  22.8 4.3 %copy-start.17 = (bf16[1,1,1,6,340,340]{5,4,3,2,1,0:T(8,128)(2,1)S(1)}, bf16[1,1,1,6,340,340]{5,4,3,2,1,0:T(8,128)(2,1)}, u32[]{:S(2)}) copy-start(bf16[1,1,1,6,340,340]{5,4,3,2,1,0:T(8,128)(2,1)} %param.8) | copy-start | bytes 4161604
  23.1 15.3 %copy-start.7 = (bf16[6,112,340]{2,1,0:T(8,128)(2,1)}, bf16[6,112,340]{2,1,0:T(8,128)(2,1)S(1)}, u32[]{:S(2)}) copy-start(bf16[6,112,340]{2,1,0:T(8,128)(2,1)S(1)} %constant_dynamic-update-slice_fusion) | copy-start | bytes 1370884
  24.7 0.8 copy-start.14
  25.5 0.8 copy-start.10
  26.2 0.8 copy-start.12
  29.4 8.8 %collective-permute-start.1 = (bf16[1,112,340]{2,1,0:T(8,128)(2,1)S(1)}, bf16[1,112,340]{2,1,0:T(8,128)(2,1)S(1)}, u32[]{:S(2)}, u32[]{:S(2)}) collective-permute-start(bf16[1,112,340]{2,1,0:T(8,128)(2,1)S(1)} %get-tuple-element.40), channel_id=1, source_target_pairs={{32,0},{64,32},{96,64},{128,96},{160,128},{192,160},{224,192},{33,... | collective-permute-start | bytes 228488 | tf_op jit(solution)/shard_map/ppermute | solution.py:19
  38.4 1.4 %copy-start.3 = (bf16[6,112,340]{2,1,0:T(8,128)(2,1)}, bf16[6,112,340]{2,1,0:T(8,128)(2,1)S(1)}, u32[]{:S(2)}) copy-start(bf16[6,112,340]{2,1,0:T(8,128)(2,1)S(1)} %constant_dynamic-update-slice_fusion.6) | copy-start | bytes 1370884
  38.4 2.9 %copy-start = (bf16[1,1,1,112,2048]{4,3,2,1,0:T(8,128)(2,1)S(1)}, bf16[1,1,1,112,2048]{4,3,2,1,0:T(8,128)(2,1)}, u32[]{:S(2)}) copy-start(bf16[1,1,1,112,2048]{4,3,2,1,0:T(8,128)(2,1)} %param.6) | copy-start | bytes 1376260
  41.3 9.0 %copy-start.4 = (bf16[6,112,340]{2,1,0:T(8,128)(2,1)S(1)}, bf16[6,112,340]{2,1,0:T(8,128)(2,1)}, u32[]{:S(2)}) copy-start(bf16[6,112,340]{2,1,0:T(8,128)(2,1)} %copy-done.3) | copy-start | bytes 1370884
  41.3 9.0 %copy-start.8 = (bf16[6,112,340]{2,1,0:T(8,128)(2,1)S(1)}, bf16[6,112,340]{2,1,0:T(8,128)(2,1)}, u32[]{:S(2)}) copy-start(bf16[6,112,340]{2,1,0:T(8,128)(2,1)} %copy-done.7) | copy-start | bytes 1370884
  41.3 9.0 %copy-start.13 = (bf16[6,112,340]{2,1,0:T(8,128)(2,1)S(1)}, bf16[6,112,340]{2,1,0:T(8,128)(2,1)}, u32[]{:S(2)}) copy-start(bf16[6,112,340]{2,1,0:T(8,128)(2,1)} %copy-done.12) | copy-start | bytes 1370884
  47.0 18.9 %collective-permute-start.6 = (bf16[1,112,340]{2,1,0:T(8,128)(2,1)S(1)}, bf16[1,112,340]{2,1,0:T(8,128)(2,1)S(1)}, u32[]{:S(2)}, u32[]{:S(2)}) collective-permute-start(bf16[1,112,340]{2,1,0:T(8,128)(2,1)S(1)} %get-tuple-element.33), channel_id=1, source_target_pairs={{0,32},{32,64},{64,96},{96,128},{128,160},{160,192},{192,224},{1,3... | collective-permute-start | bytes 228488 | tf_op jit(solution)/shard_map/ppermute | solution.py:17
  53.2 21.6 %collective-permute-start.11 = (bf16[1,112,340]{2,1,0:T(8,128)(2,1)S(1)}, bf16[1,112,340]{2,1,0:T(8,128)(2,1)S(1)}, u32[]{:S(2)}, u32[]{:S(2)}) collective-permute-start(bf16[1,112,340]{2,1,0:T(8,128)(2,1)S(1)} %get-tuple-element.29), channel_id=1, source_target_pairs={{1,0},{2,1},{3,2},{4,3},{5,4},{6,5},{7,6},{9,8},{10,9},{11,10},{12... | collective-permute-start | bytes 228488 | tf_op jit(solution)/shard_map/ppermute | solution.py:19
  55.2 19.6 %collective-permute-start.10 = (bf16[1,112,340]{2,1,0:T(8,128)(2,1)S(1)}, bf16[1,112,340]{2,1,0:T(8,128)(2,1)S(1)}, u32[]{:S(2)}, u32[]{:S(2)}) collective-permute-start(bf16[1,112,340]{2,1,0:T(8,128)(2,1)S(1)} %get-tuple-element.30), channel_id=1, source_target_pairs={{0,1},{1,2},{2,3},{3,4},{4,5},{5,6},{6,7},{8,9},{9,10},{10,11},{11... | collective-permute-start | bytes 228488 | tf_op jit(solution)/shard_map/ppermute | solution.py:17
  60.3 14.4 %collective-permute-start.8 = (bf16[1,112,340]{2,1,0:T(8,128)(2,1)S(1)}, bf16[1,112,340]{2,1,0:T(8,128)(2,1)S(1)}, u32[]{:S(2)}, u32[]{:S(2)}) collective-permute-start(bf16[1,112,340]{2,1,0:T(8,128)(2,1)S(1)} %get-tuple-element.31), channel_id=1, source_target_pairs={{0,8},{8,16},{16,24},{1,9},{9,17},{17,25},{2,10},{10,18},{18,26},{... | collective-permute-start | bytes 228488 | tf_op jit(solution)/shard_map/ppermute | solution.py:17
  62.2 12.5 %collective-permute-start.9 = (bf16[1,112,340]{2,1,0:T(8,128)(2,1)S(1)}, bf16[1,112,340]{2,1,0:T(8,128)(2,1)S(1)}, u32[]{:S(2)}, u32[]{:S(2)}) collective-permute-start(bf16[1,112,340]{2,1,0:T(8,128)(2,1)S(1)} %get-tuple-element.32), channel_id=1, source_target_pairs={{8,0},{16,8},{24,16},{9,1},{17,9},{25,17},{10,2},{18,10},{26,18},{... | collective-permute-start | bytes 228488 | tf_op jit(solution)/shard_map/ppermute | solution.py:19
  65.9 8.8 %collective-permute-start.7 = (bf16[1,112,340]{2,1,0:T(8,128)(2,1)S(1)}, bf16[1,112,340]{2,1,0:T(8,128)(2,1)S(1)}, u32[]{:S(2)}, u32[]{:S(2)}) collective-permute-start(bf16[1,112,340]{2,1,0:T(8,128)(2,1)S(1)} %get-tuple-element.34), channel_id=1, source_target_pairs={{32,0},{64,32},{96,64},{128,96},{160,128},{192,160},{224,192},{33,... | collective-permute-start | bytes 228488 | tf_op jit(solution)/shard_map/ppermute | solution.py:19
  74.8 1.6 %copy-start.5 = (bf16[6,112,340]{2,1,0:T(8,128)(2,1)}, bf16[6,112,340]{2,1,0:T(8,128)(2,1)S(1)}, u32[]{:S(2)}) copy-start(bf16[6,112,340]{2,1,0:T(8,128)(2,1)S(1)} %constant_dynamic-update-slice_fusion.18) | copy-start | bytes 1370884
  78.2 9.8 %copy-start.6 = (bf16[6,112,340]{2,1,0:T(8,128)(2,1)S(1)}, bf16[6,112,340]{2,1,0:T(8,128)(2,1)}, u32[]{:S(2)}) copy-start(bf16[6,112,340]{2,1,0:T(8,128)(2,1)} %copy-done.5) | copy-start | bytes 1370884
  78.2 9.8 %copy-start.11 = (bf16[6,112,340]{2,1,0:T(8,128)(2,1)S(1)}, bf16[6,112,340]{2,1,0:T(8,128)(2,1)}, u32[]{:S(2)}) copy-start(bf16[6,112,340]{2,1,0:T(8,128)(2,1)} %copy-done.10) | copy-start | bytes 1370884
  83.8 19.7 %collective-permute-start.12 = (bf16[1,112,340]{2,1,0:T(8,128)(2,1)S(1)}, bf16[1,112,340]{2,1,0:T(8,128)(2,1)S(1)}, u32[]{:S(2)}, u32[]{:S(2)}) collective-permute-start(bf16[1,112,340]{2,1,0:T(8,128)(2,1)S(1)} %get-tuple-element.27), channel_id=1, source_target_pairs={{0,32},{32,64},{64,96},{96,128},{128,160},{160,192},{192,224},{1,3... | collective-permute-start | bytes 228488 | tf_op jit(solution)/shard_map/ppermute | solution.py:17
  90.8 21.6 %collective-permute-start.17 = (bf16[1,112,340]{2,1,0:T(8,128)(2,1)S(1)}, bf16[1,112,340]{2,1,0:T(8,128)(2,1)S(1)}, u32[]{:S(2)}, u32[]{:S(2)}) collective-permute-start(bf16[1,112,340]{2,1,0:T(8,128)(2,1)S(1)} %get-tuple-element.23), channel_id=1, source_target_pairs={{1,0},{2,1},{3,2},{4,3},{5,4},{6,5},{7,6},{9,8},{10,9},{11,10},{12... | collective-permute-start | bytes 228488 | tf_op jit(solution)/shard_map/ppermute | solution.py:19
  92.8 19.6 %collective-permute-start.16 = (bf16[1,112,340]{2,1,0:T(8,128)(2,1)S(1)}, bf16[1,112,340]{2,1,0:T(8,128)(2,1)S(1)}, u32[]{:S(2)}, u32[]{:S(2)}) collective-permute-start(bf16[1,112,340]{2,1,0:T(8,128)(2,1)S(1)} %get-tuple-element.24), channel_id=1, source_target_pairs={{0,1},{1,2},{2,3},{3,4},{4,5},{5,6},{6,7},{8,9},{9,10},{10,11},{11... | collective-permute-start | bytes 228488 | tf_op jit(solution)/shard_map/ppermute | solution.py:17
  97.9 14.4 %collective-permute-start.14 = (bf16[1,112,340]{2,1,0:T(8,128)(2,1)S(1)}, bf16[1,112,340]{2,1,0:T(8,128)(2,1)S(1)}, u32[]{:S(2)}, u32[]{:S(2)}) collective-permute-start(bf16[1,112,340]{2,1,0:T(8,128)(2,1)S(1)} %get-tuple-element.25), channel_id=1, source_target_pairs={{0,8},{8,16},{16,24},{1,9},{9,17},{17,25},{2,10},{10,18},{18,26},{... | collective-permute-start | bytes 228488 | tf_op jit(solution)/shard_map/ppermute | solution.py:17
  99.8 12.5 %collective-permute-start.15 = (bf16[1,112,340]{2,1,0:T(8,128)(2,1)S(1)}, bf16[1,112,340]{2,1,0:T(8,128)(2,1)S(1)}, u32[]{:S(2)}, u32[]{:S(2)}) collective-permute-start(bf16[1,112,340]{2,1,0:T(8,128)(2,1)S(1)} %get-tuple-element.26), channel_id=1, source_target_pairs={{8,0},{16,8},{24,16},{9,1},{17,9},{25,17},{10,2},{18,10},{26,18},{... | collective-permute-start | bytes 228488 | tf_op jit(solution)/shard_map/ppermute | solution.py:19
  103.5 8.8 %collective-permute-start.13 = (bf16[1,112,340]{2,1,0:T(8,128)(2,1)S(1)}, bf16[1,112,340]{2,1,0:T(8,128)(2,1)S(1)}, u32[]{:S(2)}, u32[]{:S(2)}) collective-permute-start(bf16[1,112,340]{2,1,0:T(8,128)(2,1)S(1)} %get-tuple-element.28), channel_id=1, source_target_pairs={{32,0},{64,32},{96,64},{128,96},{160,128},{192,160},{224,192},{33,... | collective-permute-start | bytes 228488 | tf_op jit(solution)/shard_map/ppermute | solution.py:19
  113.0 3.3 %copy-start.15 = (bf16[6,112,340]{2,1,0:T(8,128)(2,1)S(1)}, bf16[6,112,340]{2,1,0:T(8,128)(2,1)}, u32[]{:S(2)}) copy-start(bf16[6,112,340]{2,1,0:T(8,128)(2,1)} %copy-done.14) | copy-start | bytes 1370884
  115.5 2.1 %copy-start.1 = (f32[6,340,340]{2,1,0:T(8,128)S(1)}, f32[6,340,340]{2,1,0:T(8,128)}, u32[]{:S(2)}) copy-start(f32[6,340,340]{2,1,0:T(8,128)} %fusion.32) | copy-start | bytes 8323204
  115.5 3.0 %copy-start.2 = (f32[6,340,340]{2,1,0:T(8,128)S(1)}, f32[6,340,340]{2,1,0:T(8,128)}, u32[]{:S(2)}) copy-start(f32[6,340,340]{2,1,0:T(8,128)} %fusion.34) | copy-start | bytes 8323204
where the time goes:
time: 124 us
  starting transfers between devices  60 us (48%)
  matrix products  30.8 us (25%)
  waiting for transfers between devices  15.5 us (12%)
  local copies, waits for them, and re-layouts  14.8 us (12%)
  between operations  1.44 us (1%)
    ppermute x9, starting transfers between devices, with_halo(): lax.ppermute(tail, axis, [(i, (i + 1) % count) for i in range(ends)])  32.5 us
    ppermute x9, starting transfers between devices, with_halo(): lax.ppermute(head, axis, [((i + 1) % count, i) for i in range(ends)])  27.5 us
    ppermute x9, waiting for transfers between devices, with_halo(): lax.ppermute(head, axis, [((i + 1) % count, i) for i in range(ends)])  15.5 us
    dot_general x3, matrix products, local(): jnp.dot(lowered, operator, preferred_element_type=jnp.float32)  14.7 us
    concatenate x6, local copies, waits for them, and re-layouts, local(): jnp.concatenate([fresh[number] for number in range(6)] + [hidden[:, span:...  7.39 us
    dot_general x3, matrix products, local(): jnp.einsum('kcf,kcg->kfg', inputs, stored_faces, preferred_element_type=j...  6.7 us
    unnamed x84, local copies, waits for them, and re-layouts  6.12 us
    dot_general x1, matrix products, local(): jnp.einsum('kij,kig->kjg', selector, gradient, precision=lax.Precision.HI...  5.28 us
  transfers between devices with their start and end apart: 18, of which 3 were waited for; matrix products, arithmetic and copies ran while one was open for 8% of the time, Pallas kernels for 0%

commit v1 on v0

v1 whole, which is shorter than its diff:
```python
import functools
import math

import jax
import jax.numpy as jnp
from jax import lax
from jax.experimental import pallas as pl
from jax.experimental.pallas import tpu as pltpu
from jax.sharding import PartitionSpec as P

AXES = ("gx", "gy", "gz")
ORDER = (1, 0, 4, 5, 3, 2)
VMEM = pl.BlockSpec(memory_space=pltpu.VMEM)
SMEM = pl.BlockSpec(memory_space=pltpu.SMEM)
HBM = pl.BlockSpec(memory_space=pltpu.HBM)
BF16 = jnp.bfloat16
F32 = jnp.float32
PARAMS = pltpu.CompilerParams(vmem_limit_bytes=16 * 1024 * 1024)


def vmem(array):
    return pltpu.with_memory_space_constraint(array, pltpu.VMEM)


def swap(block, axis, shift):
    count = lax.axis_size(axis)
    pairs = []
    for i in range(count):
        up = (i + shift) % 2 == 0
        pairs.append((i, (i + 1) % count if up else (i - 1) % count))
    return lax.ppermute(block, axis, pairs)


def is_even(axis):
    return lax.rem(lax.axis_index(axis), 2) == 0


def store_faces(hidden, width, sends):
    for a, axis in enumerate(AXES):
        even = is_even(axis)
        low = hidden[:, 2 * a * width : (2 * a + 1) * width]
        high = hidden[:, (2 * a + 1) * width : (2 * a + 2) * width]
        sends[2 * a][...] = jnp.where(even, high, low)
        sends[2 * a + 1][...] = jnp.where(even, low, high)


def chosen_faces(sends, recvs, flags):
    faces = []
    for a, axis in enumerate(AXES):
        even = is_even(axis)
        place = lax.axis_index(axis)
        last = lax.axis_size(axis) - 1
        for side in range(2):
            first = even if side == 1 else jnp.logical_not(even)
            own = jnp.where(first, sends[2 * a][...], sends[2 * a + 1][...])
            got = jnp.where(first, recvs[2 * a][...], recvs[2 * a + 1][...])
            outer = place == (0 if side == 0 else last)
            got = jnp.where(outer, jnp.zeros_like(got), got)
            faces.append(jnp.where(flags[2 * a + side] == 1, own, got))
    return faces


def selector(flags, node_map, k, width):
    rows = lax.broadcasted_iota(jnp.int32, (width, width), 0)
    columns = lax.broadcasted_iota(jnp.int32, (1, width), 1)
    target = jnp.where(flags[k] == 1, columns, node_map[k : k + 1, :])
    return jnp.where(rows == target, 1.0, 0.0).astype(BF16)


def fill_state(state, faces, weights, seed, tail, width):
    trace = seed.shape[1]
    edge = tail.shape[1]
    state[:, trace - edge :] = tail[...].astype(F32)
    for k in range(6):
        fresh = jnp.dot(faces[k], weights[k], preferred_element_type=F32)
        state[:, k * width : (k + 1) * width] = fresh
    return (state[...] + seed[...].astype(F32)).astype(BF16)


def first_kernel(chunk, seed, operator_hbm, *refs):
    sends, (tail, operator), (hidden, sems) = refs[:6], refs[6:8], refs[8:]
    trace = seed.shape[1]
    width = sends[0].shape[1]
    copies = []
    for j in range(trace // chunk):
        span = pl.ds(j * chunk, chunk)
        copy = pltpu.make_async_copy(operator_hbm.at[:, span], operator.at[:, span], sems.at[j])
        copy.start()
        copies.append(copy)
    for j, copy in enumerate(copies):
        copy.wait()
        span = pl.ds(j * chunk, chunk)
        hidden[:, span] = jnp.dot(seed[...], operator[:, span], preferred_element_type=F32).astype(BF16)
    store_faces(hidden, width, sends)
    tail[...] = hidden[:, trace - tail.shape[1] :]


def middle_kernel(chunk, flags, weights, seed, operator, old_tail, *refs):
    sends, recvs, outs, tail, chosen, state, hidden = (
        refs[:6], refs[6:12], refs[12:18], refs[18], refs[19], refs[20], refs[21],
    )
    trace = seed.shape[1]
    width = sends[0].shape[1]
    faces = chosen_faces(sends, recvs, flags)
    for k in range(6):
        chosen[k] = faces[k]
    lowered = fill_state(state, faces, weights, seed, old_tail, width)
    for j in range(trace // chunk):
        span = pl.ds(j * chunk, chunk)
        hidden[:, span] = jnp.dot(lowered, operator[:, span], preferred_element_type=F32).astype(BF16)
    store_faces(hidden, width, outs)
    tail[...] = hidden[:, trace - tail.shape[1] :]


def place_kernel(flags, node_map, matrices, saved, weights, choosers, stored):
    sweeps = saved.shape[0]
    columns = saved.shape[1]
    width = matrices.shape[-1]
    for k in range(6):
        choosers[k] = selector(flags, node_map, k, width)
        weights[k] = jnp.dot(choosers[k], matrices[k], preferred_element_type=F32).astype(BF16)
        for sweep in range(sweeps):
            rows = slice((sweeps - 1 - sweep) * columns, (sweeps - sweep) * columns)
            stored[k, rows, :] = saved[sweep, :, k * width : (k + 1) * width]


def transposed_product(left, right):
    return lax.dot_general(left, right, (((0,), (0,)), ((), ())), preferred_element_type=F32)


def gradient_kernel(chosen_a, chosen_b, choosers, stored, total, both):
    columns = chosen_a.shape[1]
    for k in range(6):
        both[:columns] = chosen_a[k]
        both[columns:] = chosen_b[k]
        mapped = jnp.dot(both[...], choosers[k], preferred_element_type=F32).astype(BF16)
        total[k] = transposed_product(mapped, stored[k, : 2 * columns, :])


def last_kernel(flags, weights, seed, choosers, stored, old_tail, total, *refs):
    sends, recvs, adjoint_hbm, gradient_hbm, state, adjoint, gradient, sems = (
        refs[:6], refs[6:12], refs[12], refs[13], refs[14], refs[15], refs[16], refs[17],
    )
    columns = seed.shape[0]
    width = sends[0].shape[1]
    faces = chosen_faces(sends, recvs, flags)
    adjoint[...] = fill_state(state, faces, weights, seed, old_tail, width)
    copies = [pltpu.make_async_copy(adjoint, adjoint_hbm, sems.at[6])]
    copies[0].start()
    scale = 1.0 / math.sqrt(columns)
    for k in range(6):
        mapped = jnp.dot(faces[k], choosers[k], preferred_element_type=F32).astype(BF16)
        part = total[k] + transposed_product(mapped, stored[k, 2 * columns :, :])
        gradient[k] = (part * scale).astype(BF16)
        copies.append(pltpu.make_async_copy(gradient.at[k], gradient_hbm.at[k], sems.at[k]))
        copies[-1].start()
    for copy in copies:
        copy.wait()


def exchange(sends):
    recvs = [None] * 6
    for slot in ORDER:
        recvs[slot] = swap(sends[slot], AXES[slot // 2], slot % 2)
    return recvs


def local(seed_cotangent, trace_operator, face_matrices, saved_traces, edge_flags, node_map):
    seed = vmem(seed_cotangent[0, 0, 0])
    operator_hbm = trace_operator[0, 0, 0]
    matrices = vmem(face_matrices[0, 0, 0])
    saved = vmem(saved_traces[0, 0, 0])
    flags = edge_flags[0, 0, 0]
    mapping = vmem(node_map[0, 0, 0])
    columns, trace = seed.shape
    width = matrices.shape[-1]
    sweeps = saved.shape[0]
    edge = 128
    chunk = 512
    face = pltpu.VMEM((columns, width), BF16)
    tail_shape = pltpu.VMEM((columns, edge), BF16)
    block = (6, width, width)
    row = pltpu.VMEM((columns, trace), F32)

    def cost(flops, read):
        return pl.CostEstimate(flops=int(flops), bytes_accessed=int(read), transcendentals=0)

    big = 2 * columns * trace * trace
    small = 2 * 6 * columns * width * width
    results = pl.pallas_call(
        functools.partial(first_kernel, chunk),
        out_shape=[face] * 6 + [tail_shape, pltpu.VMEM((trace, trace), BF16)],
        in_specs=[VMEM, HBM],
        out_specs=[VMEM] * 8,
        scratch_shapes=[pltpu.VMEM((columns, trace), BF16), pltpu.SemaphoreType.DMA((trace // chunk,))],
        compiler_params=PARAMS,
        cost_estimate=cost(big, 2 * trace * trace),
        name="first",
    )(seed, operator_hbm)
    sends, tail, operator = results[:6], results[6], results[7]
    weights, choosers, stored = pl.pallas_call(
        place_kernel,
        out_shape=[
            pltpu.VMEM(block, BF16),
            pltpu.VMEM(block, BF16),
            pltpu.VMEM((6, sweeps * columns, width), BF16),
        ],
        in_specs=[SMEM] + [VMEM] * 3,
        out_specs=[VMEM] * 3,
        compiler_params=PARAMS,
        cost_estimate=cost(12 * width**3, 0),
        name="place",
    )(flags, mapping, matrices, saved)
    weights, choosers, stored, operator = map(vmem, (weights, choosers, stored, operator))
    chosen = []
    for sweep in range(sweeps - 1):
        recvs = exchange(sends)
        results = pl.pallas_call(
            functools.partial(middle_kernel, chunk),
            out_shape=[face] * 6 + [tail_shape, pltpu.VMEM((6, columns, width), BF16)],
            in_specs=[SMEM] + [VMEM] * 16,
            out_specs=[VMEM] * 8,
            scratch_shapes=[row, pltpu.VMEM((columns, trace), BF16)],
            compiler_params=PARAMS,
            cost_estimate=cost(big + small, 0),
            name="middle",
        )(flags, weights, seed, operator, vmem(tail), *map(vmem, sends), *map(vmem, recvs))
        sends, tail = results[:6], results[6]
        chosen.append(vmem(results[7]))
    total = pl.pallas_call(
        gradient_kernel,
        out_shape=pltpu.VMEM(block, F32),
        in_specs=[VMEM] * 4,
        out_specs=VMEM,
        scratch_shapes=[pltpu.VMEM((2 * columns, width), BF16)],
        compiler_params=PARAMS,
        cost_estimate=cost(4 * small, 0),
        name="gradient",
    )(*chosen, choosers, stored)
    recvs = exchange(sends)
    adjoint, gradient = pl.pallas_call(
        last_kernel,
        out_shape=[
            jax.ShapeDtypeStruct((columns, trace), BF16),
            jax.ShapeDtypeStruct(block, BF16),
        ],
        in_specs=[SMEM] + [VMEM] * 18,
        out_specs=[HBM] * 2,
        scratch_shapes=[
            row,
            pltpu.VMEM((columns, trace), BF16),
            pltpu.VMEM(block, BF16),
            pltpu.SemaphoreType.DMA((7,)),
        ],
        compiler_params=PARAMS,
        cost_estimate=cost(3 * small, 0),
        name="last",
    )(flags, weights, seed, choosers, stored, vmem(tail), vmem(total), *map(vmem, sends), *map(vmem, recvs))
    return (adjoint[None, None, None], gradient[None, None, None])


def solution(mesh):
    return jax.shard_map(
        local,
        mesh=mesh,
        in_specs=(
            P("gx", "gy", "gz", None, None),
            P("gx", "gy", "gz", None, None),
            P("gx", "gy", "gz", None, None, None),
            P("gx", "gy", "gz", None, None, None),
            P("gx", "gy", "gz", None),
            P("gx", "gy", "gz", None, None),
        ),
        out_specs=(P("gx", "gy", "gz", None, None), P("gx", "gy", "gz", None, None, None)),
        check_vma=False,
    )
```

time: 124 us -> 61.9 us (0.50)
  the two profiles are of different devices: /device:TPU:120 before, /device:TPU:20 now
where the time goes in v1:
time: 61.9 us; the launch traced here: 61.8 us
  starting transfers between devices  26.1 us (42%)
  Pallas kernels  17.3 us (28%)
  waiting for transfers between devices  13 us (21%)
  local copies, waits for them, and re-layouts  4.42 us (7%)
  between operations  0.98 us (2%)
    ppermute x18, starting transfers between devices, swap(): return lax.ppermute(block, axis, pairs)  26.1 us
    ppermute x18, waiting for transfers between devices, swap(): return lax.ppermute(block, axis, pairs)  13 us
    pallas_call x2, Pallas kernels, local(): pl.pallas_call(functools.partial(middle_kernel, chunk), out_shape=[face]...  5.19 us
    unnamed x15, local copies, waits for them, and re-layouts  4.42 us
    pallas_call x1, Pallas kernels, local(): pl.pallas_call(last_kernel, out_shape=[jax.ShapeDtypeStruct((columns, tra...  4.35 us
    pallas_call x1, Pallas kernels, local(): pl.pallas_call(functools.partial(first_kernel, chunk), out_shape=[face] *...  3.29 us
    pallas_call x1, Pallas kernels, local(): pl.pallas_call(gradient_kernel, out_shape=pltpu.VMEM(block, F32), in_spec...  2.61 us
    pallas_call x1, Pallas kernels, local(): pl.pallas_call(place_kernel, out_shape=[pltpu.VMEM(block, BF16), pltpu.VM...  1.86 us
  transfers between devices with their start and end apart: 18, of which 5 were waited for; matrix products, arithmetic and copies ran while one was open for 0% of the time, Pallas kernels for 7%

profile of v1, /device:TPU:20, one launch (start us, length us, event | category | flops | bytes accessed | tf_op | source)
XLA Modules:
  0.0 61.8 jit_solution(11950847327577469129)
XLA Ops:
  0.6 0.0 copy-start
  0.6 3.4 %copy-done = bf16[1,1,1,2048,2048]{4,3,2,1,0:T(8,128)(2,1)S(1)} copy-done((bf16[1,1,1,2048,2048]{4,3,2,1,0:T(8,128)(2,1)S(1)}, bf16[1,1,1,2048,2048]{4,3,2,1,0:T(8,128)(2,1)}, u32[]{:S(2)}) %copy-start) | copy-done | bytes 8388632
  4.0 0.0 copy-start.1
  4.0 1.0 %copy-done.1 = bf16[1,1,1,112,2048]{4,3,2,1,0:T(8,128)(2,1)S(1)} copy-done((bf16[1,1,1,112,2048]{4,3,2,1,0:T(8,128)(2,1)S(1)}, bf16[1,1,1,112,2048]{4,3,2,1,0:T(8,128)(2,1)}, u32[]{:S(2)}) %copy-start.1) | copy-done | bytes 458776
  5.0 0.0 copy-start.6
  5.0 0.0 copy-start.3
  5.0 0.0 copy-start.4
  5.0 0.0 copy-start.5
  5.0 3.3 %first.1 = (bf16[112,340]{1,0:T(8,128)(2,1)S(1)}, bf16[112,340]{1,0:T(8,128)(2,1)S(1)}, bf16[112,340]{1,0:T(8,128)(2,1)S(1)}, bf16[112,340]{1,0:T(8,128)(2,1)S(1...) custom-call(bf16[112,2048]{1,0:T(8,128)(2,1)S(1)} %bitcast.11, ...), custom_call_target="tpu_custom_call" | custom-call | flops 939524096 | bytes 8388608 | tf_op jit(solution)/shard_map/first/pallas_call | solution.py:190
  8.3 0.0 copy-start.2
  8.4 0.4 collective-permute-start
  8.8 3.8 %collective-permute-start.1 = (bf16[112,340]{1,0:T(8,128)(2,1)S(1)}, bf16[112,340]{1,0:T(8,128)(2,1)S(1)}, u32[]{:S(2)}, u32[]{:S(2)}) collective-permute-start(bf16[112,340]{1,0:T(8,128)(2,1)S(1)} %get-tuple-element.37.refs_1_), channel_id=1, source_target_pairs={{0,224},{32,64},{64,32},{96,128},{128,96},{160,192},{192,160},{224... | collective-permute-start | bytes 228488 | tf_op jit(solution)/shard_map/ppermute | solution.py:31
  12.6 0.0 collective-permute-start.2
  12.6 1.4 %collective-permute-start.3 = (bf16[112,340]{1,0:T(8,128)(2,1)S(1)}, bf16[112,340]{1,0:T(8,128)(2,1)S(1)}, u32[]{:S(2)}, u32[]{:S(2)}) collective-permute-start(bf16[112,340]{1,0:T(8,128)(2,1)S(1)} %get-tuple-element.39.refs_3_), channel_id=1, source_target_pairs={{0,24},{8,16},{16,8},{24,0},{1,25},{9,17},{17,9},{25,1},{2,26},{10... | collective-permute-start | bytes 228488 | tf_op jit(solution)/shard_map/ppermute | solution.py:31
  14.0 1.9 %collective-permute-start.4 = (bf16[112,340]{1,0:T(8,128)(2,1)S(1)}, bf16[112,340]{1,0:T(8,128)(2,1)S(1)}, u32[]{:S(2)}, u32[]{:S(2)}) collective-permute-start(bf16[112,340]{1,0:T(8,128)(2,1)S(1)} %get-tuple-element.40.refs_4_), channel_id=1, source_target_pairs={{0,1},{1,0},{2,3},{3,2},{4,5},{5,4},{6,7},{7,6},{8,9},{9,8},{10,11... | collective-permute-start | bytes 228488 | tf_op jit(solution)/shard_map/ppermute | solution.py:31
  15.9 0.6 %collective-permute-done.refs_6_ = bf16[112,340]{1,0:T(8,128)(2,1)S(1)} collective-permute-done((bf16[112,340]{1,0:T(8,128)(2,1)S(1)}, bf16[112,340]{1,0:T(8,128)(2,1)S(1)}, u32[]{:S(2)}, u32[]{:S(2)}) %collective-permute-start) | collective-permute-done | bytes 76192 | tf_op jit(solution)/shard_map/ppermute | solution.py:31
  16.6 5.9 %collective-permute-start.5 = (bf16[112,340]{1,0:T(8,128)(2,1)S(1)}, bf16[112,340]{1,0:T(8,128)(2,1)S(1)}, u32[]{:S(2)}, u32[]{:S(2)}) collective-permute-start(bf16[112,340]{1,0:T(8,128)(2,1)S(1)} %get-tuple-element.41.refs_5_), channel_id=1, source_target_pairs={{0,7},{1,2},{2,1},{3,4},{4,3},{5,6},{6,5},{7,0},{8,15},{9,10},{10,... | collective-permute-start | bytes 228488 | tf_op jit(solution)/shard_map/ppermute | solution.py:31
  22.4 0.0 copy-done.6
  22.4 0.0 copy-done.3
  22.4 0.0 copy-done.4
  22.4 0.0 copy-done.5
  22.5 1.9 %place.1 = (bf16[6,340,340]{2,1,0:T(8,128)(2,1)S(1)}, bf16[6,340,340]{2,1,0:T(8,128)(2,1)S(1)}, bf16[6,336,340]{2,1,0:T(8,128)(2,1)S(1)}) custom-call(s32[6]{0:T(128)S(1)} %bitcast.18, s32[6,340]{1,0:T(8,128)S(1)} %bitcast.17, bf16[6,340,340]{2,1,0:T(8,128)(2,1)S(1)} %bitcast.15, bf16[3,112,2048]{2,1,0:T(8,128)(2,1)S(1)} %bitcast.16), custom_call_target="tpu_custom_call" | custom-call | flops 471648000 | tf_op jit(solution)/shard_map/place/pallas_call | solution.py:201
  24.3 0.0 collective-permute-done.1.refs_7_
  24.3 0.0 collective-permute-done.2.refs_8_
  24.3 0.0 collective-permute-done.3.refs_9_
  24.4 0.0 collective-permute-done.4.refs_10_
  24.4 0.5 collective-permute-done.5.refs_11_
  24.9 0.0 copy-done.2
  24.9 2.6 %middle.2 = (bf16[112,340]{1,0:T(8,128)(2,1)S(1)}, bf16[112,340]{1,0:T(8,128)(2,1)S(1)}, bf16[112,340]{1,0:T(8,128)(2,1)S(1)}, bf16[112,340]{1,0:T(8,128)(2,1)S(...) custom-call(s32[6]{0:T(128)S(1)} %bitcast.19, ...), custom_call_target="tpu_custom_call" | custom-call | flops 1094890496 | tf_op jit(solution)/shard_map/middle/pallas_call | solution.py:218
  27.5 0.1 collective-permute-start.6
  27.6 2.0 %collective-permute-start.7 = (bf16[112,340]{1,0:T(8,128)(2,1)S(1)}, bf16[112,340]{1,0:T(8,128)(2,1)S(1)}, u32[]{:S(2)}, u32[]{:S(2)}) collective-permute-start(bf16[112,340]{1,0:T(8,128)(2,1)S(1)} %get-tuple-element.44.refs_1_), channel_id=1, source_target_pairs={{0,224},{32,64},{64,32},{96,128},{128,96},{160,192},{192,160},{224... | collective-permute-start | bytes 228488 | tf_op jit(solution)/shard_map/ppermute | solution.py:31
  29.6 0.0 collective-permute-start.8
  29.6 1.4 %collective-permute-start.9 = (bf16[112,340]{1,0:T(8,128)(2,1)S(1)}, bf16[112,340]{1,0:T(8,128)(2,1)S(1)}, u32[]{:S(2)}, u32[]{:S(2)}) collective-permute-start(bf16[112,340]{1,0:T(8,128)(2,1)S(1)} %get-tuple-element.46.refs_3_), channel_id=1, source_target_pairs={{0,24},{8,16},{16,8},{24,0},{1,25},{9,17},{17,9},{25,1},{2,26},{10... | collective-permute-start | bytes 228488 | tf_op jit(solution)/shard_map/ppermute | solution.py:31
  31.0 0.0 collective-permute-start.10
  31.0 4.3 %collective-permute-done.6.refs_6_ = bf16[112,340]{1,0:T(8,128)(2,1)S(1)} collective-permute-done((bf16[112,340]{1,0:T(8,128)(2,1)S(1)}, bf16[112,340]{1,0:T(8,128)(2,1)S(1)}, u32[]{:S(2)}, u32[]{:S(2)}) %collective-permute-start.6) | collective-permute-done | bytes 76192 | tf_op jit(solution)/shard_map/ppermute | solution.py:31
  35.3 3.2 %collective-permute-start.11 = (bf16[112,340]{1,0:T(8,128)(2,1)S(1)}, bf16[112,340]{1,0:T(8,128)(2,1)S(1)}, u32[]{:S(2)}, u32[]{:S(2)}) collective-permute-start(bf16[112,340]{1,0:T(8,128)(2,1)S(1)} %get-tuple-element.48.refs_5_), channel_id=1, source_target_pairs={{0,7},{1,2},{2,1},{3,4},{4,3},{5,6},{6,5},{7,0},{8,15},{9,10},{10,... | collective-permute-start | bytes 228488 | tf_op jit(solution)/shard_map/ppermute | solution.py:31
  38.5 0.0 collective-permute-done.7.refs_7_
  38.5 0.0 collective-permute-done.8.refs_8_
  38.5 0.0 collective-permute-done.9.refs_9_
  38.6 0.0 collective-permute-done.10.refs_10_
  38.6 2.4 %collective-permute-done.11.refs_11_ = bf16[112,340]{1,0:T(8,128)(2,1)S(1)} collective-permute-done((bf16[112,340]{1,0:T(8,128)(2,1)S(1)}, bf16[112,340]{1,0:T(8,128)(2,1)S(1)}, u32[]{:S(2)}, u32[]{:S(2)}) %collective-permute-start.11) | collective-permute-done | bytes 76192 | tf_op jit(solution)/shard_map/ppermute | solution.py:31
  41.0 2.6 %middle.3 = (bf16[112,340]{1,0:T(8,128)(2,1)S(1)}, bf16[112,340]{1,0:T(8,128)(2,1)S(1)}, bf16[112,340]{1,0:T(8,128)(2,1)S(1)}, bf16[112,340]{1,0:T(8,128)(2,1)S(...) custom-call(s32[6]{0:T(128)S(1)} %bitcast.20, ...), custom_call_target="tpu_custom_call" | custom-call | flops 1094890496 | tf_op jit(solution)/shard_map/middle/pallas_call | solution.py:218
  43.6 0.1 collective-permute-start.12
  43.7 1.2 %collective-permute-start.13 = (bf16[112,340]{1,0:T(8,128)(2,1)S(1)}, bf16[112,340]{1,0:T(8,128)(2,1)S(1)}, u32[]{:S(2)}, u32[]{:S(2)}) collective-permute-start(bf16[112,340]{1,0:T(8,128)(2,1)S(1)} %get-tuple-element.53.refs_1_), channel_id=1, source_target_pairs={{0,224},{32,64},{64,32},{96,128},{128,96},{160,192},{192,160},{224... | collective-permute-start | bytes 228488 | tf_op jit(solution)/shard_map/ppermute | solution.py:31
  44.9 0.0 collective-permute-start.14
  44.9 1.4 %collective-permute-start.15 = (bf16[112,340]{1,0:T(8,128)(2,1)S(1)}, bf16[112,340]{1,0:T(8,128)(2,1)S(1)}, u32[]{:S(2)}, u32[]{:S(2)}) collective-permute-start(bf16[112,340]{1,0:T(8,128)(2,1)S(1)} %get-tuple-element.55.refs_3_), channel_id=1, source_target_pairs={{0,24},{8,16},{16,8},{24,0},{1,25},{9,17},{17,9},{25,1},{2,26},{10... | collective-permute-start | bytes 228488 | tf_op jit(solution)/shard_map/ppermute | solution.py:31
  46.3 0.0 collective-permute-start.16
  46.3 5.0 %collective-permute-done.12.refs_6_ = bf16[112,340]{1,0:T(8,128)(2,1)S(1)} collective-permute-done((bf16[112,340]{1,0:T(8,128)(2,1)S(1)}, bf16[112,340]{1,0:T(8,128)(2,1)S(1)}, u32[]{:S(2)}, u32[]{:S(2)}) %collective-permute-start.12) | collective-permute-done | bytes 76192 | tf_op jit(solution)/shard_map/ppermute | solution.py:31
  51.4 3.2 %collective-permute-start.17 = (bf16[112,340]{1,0:T(8,128)(2,1)S(1)}, bf16[112,340]{1,0:T(8,128)(2,1)S(1)}, u32[]{:S(2)}, u32[]{:S(2)}) collective-permute-start(bf16[112,340]{1,0:T(8,128)(2,1)S(1)} %get-tuple-element.57.refs_5_), channel_id=1, source_target_pairs={{0,7},{1,2},{2,1},{3,4},{4,3},{5,6},{6,5},{7,0},{8,15},{9,10},{10,... | collective-permute-start | bytes 228488 | tf_op jit(solution)/shard_map/ppermute | solution.py:31
  54.6 2.6 %gradient.1.total = f32[6,340,340]{2,1,0:T(8,128)S(1)} custom-call(bf16[6,112,340]{2,1,0:T(8,128)(2,1)S(1)} %get-tuple-element.50.chosen_a, bf16[6,112,340]{2,1,0:T(8,128)(2,1)S(1)} %get-tuple-element.51.chosen_b, bf16[6,340,340]{2,1,0:T(8,128)(2,1)S(1)} %get-tuple-element.32.choosers, bf16[6,336,340]{2,1,0:T(8,128)(2,1)S(1)} %get-tuple-element.33.stored), custom_call_target="tpu_custom_call" | custom-call | flops 621465600 | tf_op jit(solution)/shard_map/gradient/pallas_call | solution.py:230
  57.2 0.0 collective-permute-done.13.refs_7_
  57.2 0.0 collective-permute-done.14.refs_8_
  57.2 0.0 collective-permute-done.15.refs_9_
  57.2 0.0 collective-permute-done.16.refs_10_
  57.2 0.0 collective-permute-done.17.refs_11_
  57.3 4.4 %last.1 = (bf16[112,2048]{1,0:T(8,128)(2,1)}, bf16[6,340,340]{2,1,0:T(8,128)(2,1)}) custom-call(s32[6]{0:T(128)S(1)} %bitcast.21, bf16[6,340,340]{2,1,0:T(8,128)(2,1)S(1)} %get-tuple-element.31.weights, bf16[112,2048]{1,0:T(8,128)(2,1)S(1)} %bitcast.14, bf16[6,340,340]{2,1,0:T(8,128)(2,1)S(1)} %get-tuple-element.32.choosers, ...), custom_call_target="tpu_custom_call" | custom-call | flops 466099200 | tf_op jit(solution)/shard_map/last/pallas_call | solution.py:241
  (1 shorter events, 0.0 us)
Async XLA Ops:
  0.6 3.4 %copy-start = (bf16[1,1,1,2048,2048]{4,3,2,1,0:T(8,128)(2,1)S(1)}, bf16[1,1,1,2048,2048]{4,3,2,1,0:T(8,128)(2,1)}, u32[]{:S(2)}) copy-start(bf16[1,1,1,2048,2048]{4,3,2,1,0:T(8,128)(2,1)} %param.7) | copy-start | bytes 25165828
  4.0 1.0 %copy-start.1 = (bf16[1,1,1,112,2048]{4,3,2,1,0:T(8,128)(2,1)S(1)}, bf16[1,1,1,112,2048]{4,3,2,1,0:T(8,128)(2,1)}, u32[]{:S(2)}) copy-start(bf16[1,1,1,112,2048]{4,3,2,1,0:T(8,128)(2,1)} %param.6) | copy-start | bytes 1376260
  5.0 17.4 %copy-start.6 = (s32[1,1,1,6,340]{4,2,3,1,0:T(1,128)S(1)}, s32[1,1,1,6,340]{4,2,3,1,0:T(1,128)}, u32[]{:S(2)}) copy-start(s32[1,1,1,6,340]{4,2,3,1,0:T(1,128)} %param.11) | copy-start | bytes 24484
  5.0 17.4 %copy-start.3 = (bf16[1,1,1,6,340,340]{5,4,3,2,1,0:T(8,128)(2,1)S(1)}, bf16[1,1,1,6,340,340]{5,4,3,2,1,0:T(8,128)(2,1)}, u32[]{:S(2)}) copy-start(bf16[1,1,1,6,340,340]{5,4,3,2,1,0:T(8,128)(2,1)} %param.8) | copy-start | bytes 4161604
  5.0 17.4 %copy-start.4 = (bf16[1,1,1,3,112,2048]{5,4,3,2,1,0:T(8,128)(2,1)S(1)}, bf16[1,1,1,3,112,2048]{5,4,3,2,1,0:T(8,128)(2,1)}, u32[]{:S(2)}) copy-start(bf16[1,1,1,3,112,2048]{5,4,3,2,1,0:T(8,128)(2,1)} %param.9) | copy-start | bytes 4128772
  5.0 17.4 %copy-start.5 = (s32[1,1,1,6]{3,2,1,0:T(1,128)S(1)}, s32[1,1,1,6]{3,2,1,0:T(1,128)}, u32[]{:S(2)}) copy-start(s32[1,1,1,6]{3,2,1,0:T(1,128)} %param.10) | copy-start | bytes 76
  8.3 16.6 %copy-start.2 = (bf16[1,1,1,112,2048]{4,3,2,1,0:T(8,128)(2,1)S(1)}, bf16[1,1,1,112,2048]{4,3,2,1,0:T(8,128)(2,1)}, u32[]{:S(2)}) copy-start(bf16[1,1,1,112,2048]{4,3,2,1,0:T(8,128)(2,1)} %param.6) | copy-start | bytes 1376260
  8.4 8.2 %collective-permute-start = (bf16[112,340]{1,0:T(8,128)(2,1)S(1)}, bf16[112,340]{1,0:T(8,128)(2,1)S(1)}, u32[]{:S(2)}, u32[]{:S(2)}) collective-permute-start(bf16[112,340]{1,0:T(8,128)(2,1)S(1)} %get-tuple-element.36.refs_0_), channel_id=1, source_target_pairs={{0,32},{32,0},{64,96},{96,64},{128,160},{160,128},{192,224},{224,1... | collective-permute-start | bytes 228488 | tf_op jit(solution)/shard_map/ppermute | solution.py:31
  8.8 15.5 %collective-permute-start.1 = (bf16[112,340]{1,0:T(8,128)(2,1)S(1)}, bf16[112,340]{1,0:T(8,128)(2,1)S(1)}, u32[]{:S(2)}, u32[]{:S(2)}) collective-permute-start(bf16[112,340]{1,0:T(8,128)(2,1)S(1)} %get-tuple-element.37.refs_1_), channel_id=1, source_target_pairs={{0,224},{32,64},{64,32},{96,128},{128,96},{160,192},{192,160},{224... | collective-permute-start | bytes 228488 | tf_op jit(solution)/shard_map/ppermute | solution.py:31
  12.6 11.7 %collective-permute-start.2 = (bf16[112,340]{1,0:T(8,128)(2,1)S(1)}, bf16[112,340]{1,0:T(8,128)(2,1)S(1)}, u32[]{:S(2)}, u32[]{:S(2)}) collective-permute-start(bf16[112,340]{1,0:T(8,128)(2,1)S(1)} %get-tuple-element.38.refs_2_), channel_id=1, source_target_pairs={{0,8},{8,0},{16,24},{24,16},{1,9},{9,1},{17,25},{25,17},{2,10},{10... | collective-permute-start | bytes 228488 | tf_op jit(solution)/shard_map/ppermute | solution.py:31
  12.6 11.7 %collective-permute-start.3 = (bf16[112,340]{1,0:T(8,128)(2,1)S(1)}, bf16[112,340]{1,0:T(8,128)(2,1)S(1)}, u32[]{:S(2)}, u32[]{:S(2)}) collective-permute-start(bf16[112,340]{1,0:T(8,128)(2,1)S(1)} %get-tuple-element.39.refs_3_), channel_id=1, source_target_pairs={{0,24},{8,16},{16,8},{24,0},{1,25},{9,17},{17,9},{25,1},{2,26},{10... | collective-permute-start | bytes 228488 | tf_op jit(solution)/shard_map/ppermute | solution.py:31
  14.0 10.3 %collective-permute-start.4 = (bf16[112,340]{1,0:T(8,128)(2,1)S(1)}, bf16[112,340]{1,0:T(8,128)(2,1)S(1)}, u32[]{:S(2)}, u32[]{:S(2)}) collective-permute-start(bf16[112,340]{1,0:T(8,128)(2,1)S(1)} %get-tuple-element.40.refs_4_), channel_id=1, source_target_pairs={{0,1},{1,0},{2,3},{3,2},{4,5},{5,4},{6,7},{7,6},{8,9},{9,8},{10,11... | collective-permute-start | bytes 228488 | tf_op jit(solution)/shard_map/ppermute | solution.py:31
  16.6 8.3 %collective-permute-start.5 = (bf16[112,340]{1,0:T(8,128)(2,1)S(1)}, bf16[112,340]{1,0:T(8,128)(2,1)S(1)}, u32[]{:S(2)}, u32[]{:S(2)}) collective-permute-start(bf16[112,340]{1,0:T(8,128)(2,1)S(1)} %get-tuple-element.41.refs_5_), channel_id=1, source_target_pairs={{0,7},{1,2},{2,1},{3,4},{4,3},{5,6},{6,5},{7,0},{8,15},{9,10},{10,... | collective-permute-start | bytes 228488 | tf_op jit(solution)/shard_map/ppermute | solution.py:31
  27.5 7.8 %collective-permute-start.6 = (bf16[112,340]{1,0:T(8,128)(2,1)S(1)}, bf16[112,340]{1,0:T(8,128)(2,1)S(1)}, u32[]{:S(2)}, u32[]{:S(2)}) collective-permute-start(bf16[112,340]{1,0:T(8,128)(2,1)S(1)} %get-tuple-element.43.refs_0_), channel_id=1, source_target_pairs={{0,32},{32,0},{64,96},{96,64},{128,160},{160,128},{192,224},{224,1... | collective-permute-start | bytes 228488 | tf_op jit(solution)/shard_map/ppermute | solution.py:31
  27.6 10.9 %collective-permute-start.7 = (bf16[112,340]{1,0:T(8,128)(2,1)S(1)}, bf16[112,340]{1,0:T(8,128)(2,1)S(1)}, u32[]{:S(2)}, u32[]{:S(2)}) collective-permute-start(bf16[112,340]{1,0:T(8,128)(2,1)S(1)} %get-tuple-element.44.refs_1_), channel_id=1, source_target_pairs={{0,224},{32,64},{64,32},{96,128},{128,96},{160,192},{192,160},{224... | collective-permute-start | bytes 228488 | tf_op jit(solution)/shard_map/ppermute | solution.py:31
  29.6 8.9 %collective-permute-start.8 = (bf16[112,340]{1,0:T(8,128)(2,1)S(1)}, bf16[112,340]{1,0:T(8,128)(2,1)S(1)}, u32[]{:S(2)}, u32[]{:S(2)}) collective-permute-start(bf16[112,340]{1,0:T(8,128)(2,1)S(1)} %get-tuple-element.45.refs_2_), channel_id=1, source_target_pairs={{0,8},{8,0},{16,24},{24,16},{1,9},{9,1},{17,25},{25,17},{2,10},{10... | collective-permute-start | bytes 228488 | tf_op jit(solution)/shard_map/ppermute | solution.py:31
  29.6 8.9 %collective-permute-start.9 = (bf16[112,340]{1,0:T(8,128)(2,1)S(1)}, bf16[112,340]{1,0:T(8,128)(2,1)S(1)}, u32[]{:S(2)}, u32[]{:S(2)}) collective-permute-start(bf16[112,340]{1,0:T(8,128)(2,1)S(1)} %get-tuple-element.46.refs_3_), channel_id=1, source_target_pairs={{0,24},{8,16},{16,8},{24,0},{1,25},{9,17},{17,9},{25,1},{2,26},{10... | collective-permute-start | bytes 228488 | tf_op jit(solution)/shard_map/ppermute | solution.py:31
  31.0 7.5 %collective-permute-start.10 = (bf16[112,340]{1,0:T(8,128)(2,1)S(1)}, bf16[112,340]{1,0:T(8,128)(2,1)S(1)}, u32[]{:S(2)}, u32[]{:S(2)}) collective-permute-start(bf16[112,340]{1,0:T(8,128)(2,1)S(1)} %get-tuple-element.47.refs_4_), channel_id=1, source_target_pairs={{0,1},{1,0},{2,3},{3,2},{4,5},{5,4},{6,7},{7,6},{8,9},{9,8},{10,11... | collective-permute-start | bytes 228488 | tf_op jit(solution)/shard_map/ppermute | solution.py:31
  35.3 5.7 %collective-permute-start.11 = (bf16[112,340]{1,0:T(8,128)(2,1)S(1)}, bf16[112,340]{1,0:T(8,128)(2,1)S(1)}, u32[]{:S(2)}, u32[]{:S(2)}) collective-permute-start(bf16[112,340]{1,0:T(8,128)(2,1)S(1)} %get-tuple-element.48.refs_5_), channel_id=1, source_target_pairs={{0,7},{1,2},{2,1},{3,4},{4,3},{5,6},{6,5},{7,0},{8,15},{9,10},{10,... | collective-permute-start | bytes 228488 | tf_op jit(solution)/shard_map/ppermute | solution.py:31
  43.6 7.7 %collective-permute-start.12 = (bf16[112,340]{1,0:T(8,128)(2,1)S(1)}, bf16[112,340]{1,0:T(8,128)(2,1)S(1)}, u32[]{:S(2)}, u32[]{:S(2)}) collective-permute-start(bf16[112,340]{1,0:T(8,128)(2,1)S(1)} %get-tuple-element.52.refs_0_), channel_id=1, source_target_pairs={{0,32},{32,0},{64,96},{96,64},{128,160},{160,128},{192,224},{224,1... | collective-permute-start | bytes 228488 | tf_op jit(solution)/shard_map/ppermute | solution.py:31
  43.7 13.5 %collective-permute-start.13 = (bf16[112,340]{1,0:T(8,128)(2,1)S(1)}, bf16[112,340]{1,0:T(8,128)(2,1)S(1)}, u32[]{:S(2)}, u32[]{:S(2)}) collective-permute-start(bf16[112,340]{1,0:T(8,128)(2,1)S(1)} %get-tuple-element.53.refs_1_), channel_id=1, source_target_pairs={{0,224},{32,64},{64,32},{96,128},{128,96},{160,192},{192,160},{224... | collective-permute-start | bytes 228488 | tf_op jit(solution)/shard_map/ppermute | solution.py:31
  44.9 12.3 %collective-permute-start.14 = (bf16[112,340]{1,0:T(8,128)(2,1)S(1)}, bf16[112,340]{1,0:T(8,128)(2,1)S(1)}, u32[]{:S(2)}, u32[]{:S(2)}) collective-permute-start(bf16[112,340]{1,0:T(8,128)(2,1)S(1)} %get-tuple-element.54.refs_2_), channel_id=1, source_target_pairs={{0,8},{8,0},{16,24},{24,16},{1,9},{9,1},{17,25},{25,17},{2,10},{10... | collective-permute-start | bytes 228488 | tf_op jit(solution)/shard_map/ppermute | solution.py:31
  44.9 12.3 %collective-permute-start.15 = (bf16[112,340]{1,0:T(8,128)(2,1)S(1)}, bf16[112,340]{1,0:T(8,128)(2,1)S(1)}, u32[]{:S(2)}, u32[]{:S(2)}) collective-permute-start(bf16[112,340]{1,0:T(8,128)(2,1)S(1)} %get-tuple-element.55.refs_3_), channel_id=1, source_target_pairs={{0,24},{8,16},{16,8},{24,0},{1,25},{9,17},{17,9},{25,1},{2,26},{10... | collective-permute-start | bytes 228488 | tf_op jit(solution)/shard_map/ppermute | solution.py:31
  46.3 10.9 %collective-permute-start.16 = (bf16[112,340]{1,0:T(8,128)(2,1)S(1)}, bf16[112,340]{1,0:T(8,128)(2,1)S(1)}, u32[]{:S(2)}, u32[]{:S(2)}) collective-permute-start(bf16[112,340]{1,0:T(8,128)(2,1)S(1)} %get-tuple-element.56.refs_4_), channel_id=1, source_target_pairs={{0,1},{1,0},{2,3},{3,2},{4,5},{5,4},{6,7},{7,6},{8,9},{9,8},{10,11... | collective-permute-start | bytes 228488 | tf_op jit(solution)/shard_map/ppermute | solution.py:31
  51.4 5.9 %collective-permute-start.17 = (bf16[112,340]{1,0:T(8,128)(2,1)S(1)}, bf16[112,340]{1,0:T(8,128)(2,1)S(1)}, u32[]{:S(2)}, u32[]{:S(2)}) collective-permute-start(bf16[112,340]{1,0:T(8,128)(2,1)S(1)} %get-tuple-element.57.refs_5_), channel_id=1, source_target_pairs={{0,7},{1,2},{2,1},{3,4},{4,3},{5,6},{6,5},{7,0},{8,15},{9,10},{10,... | collective-permute-start | bytes 228488 | tf_op jit(solution)/shard_map/ppermute | solution.py:31

commit v2 on v1

--- a/solution.py
+++ b/solution.py
@@ -18,6 +18,10 @@
 PARAMS = pltpu.CompilerParams(vmem_limit_bytes=16 * 1024 * 1024)
 
 
+def hbm(array):
+    return pltpu.with_memory_space_constraint(array, pltpu.HBM)
+
+
 def vmem(array):
     return pltpu.with_memory_space_constraint(array, pltpu.VMEM)
 
@@ -35,13 +39,13 @@
     return lax.rem(lax.axis_index(axis), 2) == 0
 
 
-def store_faces(hidden, width, sends):
-    for a, axis in enumerate(AXES):
-        even = is_even(axis)
+def store_faces(hidden, width, axis_numbers, sends):
+    for n, a in enumerate(axis_numbers):
+        even = is_even(AXES[a])
         low = hidden[:, 2 * a * width : (2 * a + 1) * width]
         high = hidden[:, (2 * a + 1) * width : (2 * a + 2) * width]
-        sends[2 * a][...] = jnp.where(even, high, low)
-        sends[2 * a + 1][...] = jnp.where(even, low, high)
+        sends[2 * n][...] = jnp.where(even, high, low)
+        sends[2 * n + 1][...] = jnp.where(even, low, high)
 
 
 def chosen_faces(sends, recvs, flags):
@@ -77,39 +81,55 @@
     return (state[...] + seed[...].astype(F32)).astype(BF16)
 
 
-def first_kernel(chunk, seed, operator_hbm, *refs):
-    sends, (tail, operator), (hidden, sems) = refs[:6], refs[6:8], refs[8:]
-    trace = seed.shape[1]
-    width = sends[0].shape[1]
-    copies = []
-    for j in range(trace // chunk):
+def first_kernel(chunk, seed_hbm, operator_hbm, send_a, send_b, joint, seed, operator, hidden, sems):
+    width = send_a.shape[1]
+    shared = joint.shape[1]
+    head = operator.shape[1]
+    copies = [pltpu.make_async_copy(seed_hbm, seed, sems.at[0])]
+    for j in range(head // chunk):
         span = pl.ds(j * chunk, chunk)
-        copy = pltpu.make_async_copy(operator_hbm.at[:, span], operator.at[:, span], sems.at[j])
+        copies.append(
+            pltpu.make_async_copy(operator_hbm.at[:, span], operator.at[:, span], sems.at[j + 1])
+        )
+    for copy in copies:
         copy.start()
-        copies.append(copy)
-    for j, copy in enumerate(copies):
+    copies[0].wait()
+    for j, copy in enumerate(copies[1:]):
         copy.wait()
         span = pl.ds(j * chunk, chunk)
         hidden[:, span] = jnp.dot(seed[...], operator[:, span], preferred_element_type=F32).astype(BF16)
-    store_faces(hidden, width, sends)
+    store_faces(hidden, width, (0,), (send_a, send_b))
+    joint[...] = hidden[:, head - shared :]
+
+
+def rest_kernel(chunk, head, state, operator, joint, *refs):
+    sends, tail, hidden = refs[:4], refs[4], refs[5]
+    width = sends[0].shape[1]
+    trace = state.shape[1]
+    hidden[:, head - joint.shape[1] : head] = joint[...]
+    for start in range(head, trace, chunk):
+        span = pl.ds(start, chunk)
+        hidden[:, span] = jnp.dot(state[...], operator[:, span], preferred_element_type=F32).astype(BF16)
+    store_faces(hidden, width, (1, 2), sends)
     tail[...] = hidden[:, trace - tail.shape[1] :]
 
 
-def middle_kernel(chunk, flags, weights, seed, operator, old_tail, *refs):
-    sends, recvs, outs, tail, chosen, state, hidden = (
-        refs[:6], refs[6:12], refs[12:18], refs[18], refs[19], refs[20], refs[21],
+def middle_kernel(chunk, head, flags, weights, seed, operator, *refs):
+    refs = refs[7:13] + refs[:6] + refs[14:] + (refs[6],)
+    tail = refs[-1]
+    sends, recvs, outs, joint, chosen, lowered, state, hidden = (
+        refs[:6], refs[6:12], refs[12:14], refs[14], refs[15], refs[16], refs[17], refs[18],
     )
-    trace = seed.shape[1]
     width = sends[0].shape[1]
-    faces = chosen_faces(sends, recvs, flags)
+    faces = chosen_faces(sends, by_slot(recvs), flags)
     for k in range(6):
         chosen[k] = faces[k]
-    lowered = fill_state(state, faces, weights, seed, old_tail, width)
-    for j in range(trace // chunk):
-        span = pl.ds(j * chunk, chunk)
-        hidden[:, span] = jnp.dot(lowered, operator[:, span], preferred_element_type=F32).astype(BF16)
-    store_faces(hidden, width, outs)
-    tail[...] = hidden[:, trace - tail.shape[1] :]
+    lowered[...] = fill_state(state, faces, weights, seed, tail, width)
+    for start in range(0, head, chunk):
+        span = pl.ds(start, chunk)
+        hidden[:, span] = jnp.dot(lowered[...], operator[:, span], preferred_element_type=F32).astype(BF16)
+    store_faces(hidden, width, (0,), outs)
+    joint[...] = hidden[:, head - joint.shape[1] : head]
 
 
 def place_kernel(flags, node_map, matrices, saved, weights, choosers, stored):
@@ -137,13 +157,15 @@
         total[k] = transposed_product(mapped, stored[k, : 2 * columns, :])
 
 
-def last_kernel(flags, weights, seed, choosers, stored, old_tail, total, *refs):
+def last_kernel(flags, weights, seed, choosers, stored, *refs):
+    old_tail, total = refs[6:8]
+    refs = refs[8:14] + refs[:6] + refs[15:]
     sends, recvs, adjoint_hbm, gradient_hbm, state, adjoint, gradient, sems = (
         refs[:6], refs[6:12], refs[12], refs[13], refs[14], refs[15], refs[16], refs[17],
     )
     columns = seed.shape[0]
     width = sends[0].shape[1]
-    faces = chosen_faces(sends, recvs, flags)
+    faces = chosen_faces(sends, by_slot(recvs), flags)
     adjoint[...] = fill_state(state, faces, weights, seed, old_tail, width)
     copies = [pltpu.make_async_copy(adjoint, adjoint_hbm, sems.at[6])]
     copies[0].start()
@@ -158,25 +180,28 @@
         copy.wait()
 
 
-def exchange(sends):
-    recvs = [None] * 6
-    for slot in ORDER:
-        recvs[slot] = swap(sends[slot], AXES[slot // 2], slot % 2)
-    return recvs
+def exchange(sends, slots):
+    return [vmem(swap(send, AXES[slot // 2], slot % 2)) for send, slot in zip(sends, slots)]
+
+
+def by_slot(recvs):
+    return [recvs[ORDER.index(slot)] for slot in range(6)]
 
 
 def local(seed_cotangent, trace_operator, face_matrices, saved_traces, edge_flags, node_map):
-    seed = vmem(seed_cotangent[0, 0, 0])
-    operator_hbm = trace_operator[0, 0, 0]
+    seed_hbm = hbm(seed_cotangent[0, 0, 0])
+    operator_hbm = hbm(trace_operator[0, 0, 0])
+    operator = vmem(trace_operator[0, 0, 0])
     matrices = vmem(face_matrices[0, 0, 0])
     saved = vmem(saved_traces[0, 0, 0])
     flags = edge_flags[0, 0, 0]
     mapping = vmem(node_map[0, 0, 0])
-    columns, trace = seed.shape
+    columns, trace = seed_hbm.shape
     width = matrices.shape[-1]
     sweeps = saved.shape[0]
     edge = 128
-    chunk = 512
+    chunk = 256
+    head = -(-2 * width // chunk) * chunk
     face = pltpu.VMEM((columns, width), BF16)
     tail_shape = pltpu.VMEM((columns, edge), BF16)
     block = (6, width, width)
@@ -187,17 +212,40 @@
 
     big = 2 * columns * trace * trace
     small = 2 * 6 * columns * width * width
-    results = pl.pallas_call(
+    def rest(state, joint):
+        results = pl.pallas_call(
+            functools.partial(rest_kernel, chunk, head),
+            out_shape=[face] * 4 + [tail_shape],
+            in_specs=[VMEM] * 3,
+            out_specs=[VMEM] * 5,
+            scratch_shapes=[lowered_scratch],
+            compiler_params=PARAMS,
+            cost_estimate=cost(big * (trace - head) // trace, 0),
+            name="rest",
+        )(vmem(state), operator, vmem(joint))
+        return list(results[:4]), results[4]
+
+    lowered_scratch = pltpu.VMEM((columns, trace), BF16)
+    joint_shape = pltpu.VMEM((columns, head - 2 * width // 128 * 128), BF16)
+    *sends, joint, seed = pl.pallas_call(
         functools.partial(first_kernel, chunk),
-        out_shape=[face] * 6 + [tail_shape, pltpu.VMEM((trace, trace), BF16)],
-        in_specs=[VMEM, HBM],
-        out_specs=[VMEM] * 8,
-        scratch_shapes=[pltpu.VMEM((columns, trace), BF16), pltpu.SemaphoreType.DMA((trace // chunk,))],
+        out_shape=[face, face, joint_shape, pltpu.VMEM((columns, trace), BF16)],
+        in_specs=[HBM] * 2,
+        out_specs=[VMEM] * 4,
+        scratch_shapes=[
+            pltpu.VMEM((trace, head), BF16),
+            pltpu.VMEM((columns, head), BF16),
+            pltpu.SemaphoreType.DMA((head // chunk + 1,)),
+        ],
         compiler_params=PARAMS,
-        cost_estimate=cost(big, 2 * trace * trace),
+        cost_estimate=cost(big * head // trace, 2 * trace * head),
         name="first",
-    )(seed, operator_hbm)
-    sends, tail, operator = results[:6], results[6], results[7]
+    )(seed_hbm, operator_hbm)
+    state = seed = vmem(seed)
+    recvs = exchange([sends[slot] for slot in ORDER[:2]], ORDER[:2])
+    others, tail = rest(seed, joint)
+    sends = sends + others
+    recvs = recvs + exchange([sends[slot] for slot in ORDER[2:]], ORDER[2:])
     weights, choosers, stored = pl.pallas_call(
         place_kernel,
         out_shape=[
@@ -211,22 +259,30 @@
         cost_estimate=cost(12 * width**3, 0),
         name="place",
     )(flags, mapping, matrices, saved)
-    weights, choosers, stored, operator = map(vmem, (weights, choosers, stored, operator))
+    weights, choosers, stored = map(vmem, (weights, choosers, stored))
     chosen = []
     for sweep in range(sweeps - 1):
-        recvs = exchange(sends)
-        results = pl.pallas_call(
-            functools.partial(middle_kernel, chunk),
-            out_shape=[face] * 6 + [tail_shape, pltpu.VMEM((6, columns, width), BF16)],
-            in_specs=[SMEM] + [VMEM] * 16,
-            out_specs=[VMEM] * 8,
-            scratch_shapes=[row, pltpu.VMEM((columns, trace), BF16)],
+        *sends, joint, picked, state = pl.pallas_call(
+            functools.partial(middle_kernel, chunk, head),
+            out_shape=[
+                face,
+                face,
+                joint_shape,
+                pltpu.VMEM((6, columns, width), BF16),
+                pltpu.VMEM((columns, trace), BF16),
+            ],
+            in_specs=[SMEM] + [VMEM] * 17,
+            out_specs=[VMEM] * 5,
+            scratch_shapes=[row, pltpu.VMEM((columns, head), BF16)],
             compiler_params=PARAMS,
-            cost_estimate=cost(big + small, 0),
+            cost_estimate=cost(big * head // trace + small, 0),
             name="middle",
-        )(flags, weights, seed, operator, vmem(tail), *map(vmem, sends), *map(vmem, recvs))
-        sends, tail = results[:6], results[6]
-        chosen.append(vmem(results[7]))
+        )(flags, weights, seed, operator, *recvs, vmem(tail), *map(vmem, sends), vmem(state))
+        chosen.append(vmem(picked))
+        recvs = exchange([sends[slot] for slot in ORDER[:2]], ORDER[:2])
+        others, tail = rest(state, joint)
+        sends = sends + others
+        recvs = recvs + exchange([sends[slot] for slot in ORDER[2:]], ORDER[2:])
     total = pl.pallas_call(
         gradient_kernel,
         out_shape=pltpu.VMEM(block, F32),
@@ -237,14 +293,13 @@
         cost_estimate=cost(4 * small, 0),
         name="gradient",
     )(*chosen, choosers, stored)
-    recvs = exchange(sends)
     adjoint, gradient = pl.pallas_call(
         last_kernel,
         out_shape=[
             jax.ShapeDtypeStruct((columns, trace), BF16),
             jax.ShapeDtypeStruct(block, BF16),
         ],
-        in_specs=[SMEM] + [VMEM] * 18,
+        in_specs=[SMEM] + [VMEM] * 19,
         out_specs=[HBM] * 2,
         scratch_shapes=[
             row,
@@ -255,7 +310,7 @@
         compiler_params=PARAMS,
         cost_estimate=cost(3 * small, 0),
         name="last",
-    )(flags, weights, seed, choosers, stored, vmem(tail), vmem(total), *map(vmem, sends), *map(vmem, recvs))
+    )(flags, weights, seed, choosers, stored, *recvs, vmem(tail), vmem(total), *map(vmem, sends), vmem(state))
     return (adjoint[None, None, None], gradient[None, None, None])
 
 

time: 61.9 us -> 54.1 us (0.87)
  the two profiles are of different devices: /device:TPU:20 before, /device:TPU:1 now
where the time goes in v2:
time: 54.1 us; the launch traced here: 54 us
  starting transfers between devices  30.7 us (57%)
  Pallas kernels  18.9 us (35%)
  waiting for transfers between devices  3.34 us (6%)
  between operations  0.99 us (2%)
    ppermute x18, starting transfers between devices, swap(): return lax.ppermute(block, axis, pairs)  30.7 us
    pallas_call x1, Pallas kernels, local(): pl.pallas_call(last_kernel, out_shape=[jax.ShapeDtypeStruct((columns, tra...  4.35 us
    pallas_call x2, Pallas kernels, local(): pl.pallas_call(functools.partial(middle_kernel, chunk, head), out_shape=[...  3.89 us
    pallas_call x3, Pallas kernels, rest(): pl.pallas_call(functools.partial(rest_kernel, chunk, head), out_shape=[fa...  3.37 us
    ppermute x18, waiting for transfers between devices, swap(): return lax.ppermute(block, axis, pairs)  3.34 us
    pallas_call x1, Pallas kernels, local(): pl.pallas_call(functools.partial(first_kernel, chunk), out_shape=[face, f...  2.8 us
    pallas_call x1, Pallas kernels, local(): pl.pallas_call(gradient_kernel, out_shape=pltpu.VMEM(block, F32), in_spec...  2.62 us
    pallas_call x1, Pallas kernels, local(): pl.pallas_call(place_kernel, out_shape=[pltpu.VMEM(block, BF16), pltpu.VM...  1.86 us
  transfers between devices with their start and end apart: 18, of which 4 were waited for; matrix products, arithmetic and copies ran while one was open for 0% of the time, Pallas kernels for 15%

profile of v2, /device:TPU:1, one launch (start us, length us, event | category | flops | bytes accessed | tf_op | source)
XLA Modules:
  0.0 54.0 jit_solution(7407253219195585395)
XLA Ops:
  0.6 0.0 copy-start
  0.6 2.8 %first.1 = (bf16[112,340]{1,0:T(8,128)(2,1)S(1)}, bf16[112,340]{1,0:T(8,128)(2,1)S(1)}, bf16[112,128]{1,0:T(8,128)(2,1)S(1)}, bf16[112,2048]{1,0:T(8,128)(2,1)S(1)}) custom-call(bf16[112,2048]{1,0:T(8,128)(2,1)} %bitcast.23, bf16[2048,2048]{1,0:T(8,128)(2,1)} %bitcast.10), custom_call_target="tpu_custom_call" | custom-call | flops 352321536 | bytes 3145728 | tf_op jit(solution)/shard_map/first/pallas_call | solution.py:230
  3.4 6.0 %collective-permute-start = (bf16[112,340]{1,0:T(8,128)(2,1)S(1)}, bf16[112,340]{1,0:T(8,128)(2,1)S(1)}, u32[]{:S(2)}, u32[]{:S(2)}) collective-permute-start(bf16[112,340]{1,0:T(8,128)(2,1)S(1)} %get-tuple-element.40.refs_8_), channel_id=1, source_target_pairs={{0,224},{32,64},{64,32},{96,128},{128,96},{160,192},{192,160},{224... | collective-permute-start | bytes 228488 | tf_op jit(solution)/shard_map/ppermute | solution.py:35
  9.5 0.0 collective-permute-start.1
  9.5 0.0 copy-done
  9.5 0.0 copy-start.4
  9.5 0.0 copy-start.1
  9.5 0.0 copy-start.2
  9.5 0.0 copy-start.3
  9.5 1.2 %rest.3 = (bf16[112,340]{1,0:T(8,128)(2,1)S(1)}, bf16[112,340]{1,0:T(8,128)(2,1)S(1)}, bf16[112,340]{1,0:T(8,128)(2,1)S(1)}, bf16[112,340]{1,0:T(8,128)(2,1)S(1)}, bf16[112,128]{1,0:T(8,128)(2,1)S(1)}) custom-call(bf16[112,2048]{1,0:T(8,128)(2,1)S(1)} %get-tuple-element.37.state.seed.refs_13_, bf16[2048,2048]{1,0:T(8,128)(2,1)S(1)} %bitcast.11, ...), custom_call_target="tpu_custom_call" | custom-call | flops 587202560 | tf_op jit(solution)/shard_map/rest/pallas_call | solution.py:216
  10.7 1.7 %collective-permute-start.2 = (bf16[112,340]{1,0:T(8,128)(2,1)S(1)}, bf16[112,340]{1,0:T(8,128)(2,1)S(1)}, u32[]{:S(2)}, u32[]{:S(2)}) collective-permute-start(bf16[112,340]{1,0:T(8,128)(2,1)S(1)} %get-tuple-element.43.refs_11_), channel_id=1, source_target_pairs={{0,1},{1,0},{2,3},{3,2},{4,5},{5,4},{6,7},{7,6},{8,9},{9,8},{10,11... | collective-permute-start | bytes 228488 | tf_op jit(solution)/shard_map/ppermute | solution.py:35
  12.4 4.7 %collective-permute-start.3 = (bf16[112,340]{1,0:T(8,128)(2,1)S(1)}, bf16[112,340]{1,0:T(8,128)(2,1)S(1)}, u32[]{:S(2)}, u32[]{:S(2)}) collective-permute-start(bf16[112,340]{1,0:T(8,128)(2,1)S(1)} %get-tuple-element.44.refs_12_), channel_id=1, source_target_pairs={{0,7},{1,2},{2,1},{3,4},{4,3},{5,6},{6,5},{7,0},{8,15},{9,10},{10,... | collective-permute-start | bytes 228488 | tf_op jit(solution)/shard_map/ppermute | solution.py:35
  17.1 1.8 %collective-permute-start.4 = (bf16[112,340]{1,0:T(8,128)(2,1)S(1)}, bf16[112,340]{1,0:T(8,128)(2,1)S(1)}, u32[]{:S(2)}, u32[]{:S(2)}) collective-permute-start(bf16[112,340]{1,0:T(8,128)(2,1)S(1)} %get-tuple-element.45.refs_10_), channel_id=1, source_target_pairs={{0,24},{8,16},{16,8},{24,0},{1,25},{9,17},{17,9},{25,1},{2,26},{10... | collective-permute-start | bytes 228488 | tf_op jit(solution)/shard_map/ppermute | solution.py:35
  18.9 0.0 collective-permute-done.refs_0_
  18.9 0.0 collective-permute-start.5
  18.9 0.0 copy-done.4
  18.9 0.0 copy-done.1
  18.9 0.0 copy-done.2
  18.9 0.0 copy-done.3
  18.9 1.9 %place.1 = (bf16[6,340,340]{2,1,0:T(8,128)(2,1)S(1)}, bf16[6,340,340]{2,1,0:T(8,128)(2,1)S(1)}, bf16[6,336,340]{2,1,0:T(8,128)(2,1)S(1)}) custom-call(s32[6]{0:T(128)S(1)} %bitcast.19, s32[6,340]{1,0:T(8,128)S(1)} %bitcast.18, bf16[6,340,340]{2,1,0:T(8,128)(2,1)S(1)} %bitcast.16, bf16[3,112,2048]{2,1,0:T(8,128)(2,1)S(1)} %bitcast.17), custom_call_target="tpu_custom_call" | custom-call | flops 471648000 | tf_op jit(solution)/shard_map/place/pallas_call | solution.py:249
  20.8 0.0 collective-permute-done.1.refs_1_
  20.8 0.0 collective-permute-done.2.refs_2_
  20.8 0.0 collective-permute-done.3.refs_3_
  20.8 0.7 %collective-permute-done.4.refs_4_ = bf16[112,340]{1,0:T(8,128)(2,1)S(1)} collective-permute-done((bf16[112,340]{1,0:T(8,128)(2,1)S(1)}, bf16[112,340]{1,0:T(8,128)(2,1)S(1)}, u32[]{:S(2)}, u32[]{:S(2)}) %collective-permute-start.4) | collective-permute-done | bytes 76192 | tf_op jit(solution)/shard_map/ppermute | solution.py:35
  21.5 0.0 collective-permute-done.5.refs_5_
  21.5 2.0 %middle.2 = (bf16[112,340]{1,0:T(8,128)(2,1)S(1)}, bf16[112,340]{1,0:T(8,128)(2,1)S(1)}, bf16[112,128]{1,0:T(8,128)(2,1)S(1)}, bf16[6,112,340]{2,1,0:T(8,128)(2,1)S(1)}, bf16[112,2048]{1,0:T(8,128)(2,1)S(1)}) custom-call(s32[6]{0:T(128)S(1)} %bitcast.20, bf16[6,340,340]{2,1,0:T(8,128)(2,1)S(1)} %get-tuple-element.36.weights, ...), custom_call_target="tpu_custom_call" | custom-call | flops 507687936 | tf_op jit(solution)/shard_map/middle/pallas_call | solution.py:265
  23.5 4.8 %collective-permute-start.6 = (bf16[112,340]{1,0:T(8,128)(2,1)S(1)}, bf16[112,340]{1,0:T(8,128)(2,1)S(1)}, u32[]{:S(2)}, u32[]{:S(2)}) collective-permute-start(bf16[112,340]{1,0:T(8,128)(2,1)S(1)} %get-tuple-element.48.refs_8_), channel_id=1, source_target_pairs={{0,224},{32,64},{64,32},{96,128},{128,96},{160,192},{192,160},{224... | collective-permute-start | bytes 228488 | tf_op jit(solution)/shard_map/ppermute | solution.py:35
  28.2 0.0 collective-permute-start.7
  28.2 1.1 %rest.4 = (bf16[112,340]{1,0:T(8,128)(2,1)S(1)}, bf16[112,340]{1,0:T(8,128)(2,1)S(1)}, bf16[112,340]{1,0:T(8,128)(2,1)S(1)}, bf16[112,340]{1,0:T(8,128)(2,1)S(1)}, bf16[112,128]{1,0:T(8,128)(2,1)S(1)}) custom-call(bf16[112,2048]{1,0:T(8,128)(2,1)S(1)} %get-tuple-element.50.state.refs_13_, bf16[2048,2048]{1,0:T(8,128)(2,1)S(1)} %bitcast.13, ...), custom_call_target="tpu_custom_call" | custom-call | flops 587202560 | tf_op jit(solution)/shard_map/rest/pallas_call | solution.py:216
  29.4 0.1 collective-permute-start.8
  29.5 1.4 %collective-permute-start.9 = (bf16[112,340]{1,0:T(8,128)(2,1)S(1)}, bf16[112,340]{1,0:T(8,128)(2,1)S(1)}, u32[]{:S(2)}, u32[]{:S(2)}) collective-permute-start(bf16[112,340]{1,0:T(8,128)(2,1)S(1)} %get-tuple-element.53.refs_12_), channel_id=1, source_target_pairs={{0,7},{1,2},{2,1},{3,4},{4,3},{5,6},{6,5},{7,0},{8,15},{9,10},{10,... | collective-permute-start | bytes 228488 | tf_op jit(solution)/shard_map/ppermute | solution.py:35
  30.9 1.6 %collective-permute-start.10 = (bf16[112,340]{1,0:T(8,128)(2,1)S(1)}, bf16[112,340]{1,0:T(8,128)(2,1)S(1)}, u32[]{:S(2)}, u32[]{:S(2)}) collective-permute-start(bf16[112,340]{1,0:T(8,128)(2,1)S(1)} %get-tuple-element.54.refs_10_), channel_id=1, source_target_pairs={{0,24},{8,16},{16,8},{24,0},{1,25},{9,17},{17,9},{25,1},{2,26},{10... | collective-permute-start | bytes 228488 | tf_op jit(solution)/shard_map/ppermute | solution.py:35
  32.5 0.0 collective-permute-done.6.refs_0_
  32.5 0.3 collective-permute-start.11
  32.8 0.3 collective-permute-done.7.refs_1_
  33.1 0.0 collective-permute-done.8.refs_2_
  33.1 1.3 %collective-permute-done.9.refs_3_ = bf16[112,340]{1,0:T(8,128)(2,1)S(1)} collective-permute-done((bf16[112,340]{1,0:T(8,128)(2,1)S(1)}, bf16[112,340]{1,0:T(8,128)(2,1)S(1)}, u32[]{:S(2)}, u32[]{:S(2)}) %collective-permute-start.9) | collective-permute-done | bytes 76192 | tf_op jit(solution)/shard_map/ppermute | solution.py:35
  34.4 1.0 %collective-permute-done.10.refs_4_ = bf16[112,340]{1,0:T(8,128)(2,1)S(1)} collective-permute-done((bf16[112,340]{1,0:T(8,128)(2,1)S(1)}, bf16[112,340]{1,0:T(8,128)(2,1)S(1)}, u32[]{:S(2)}, u32[]{:S(2)}) %collective-permute-start.10) | collective-permute-done | bytes 76192 | tf_op jit(solution)/shard_map/ppermute | solution.py:35
  35.4 0.0 collective-permute-done.11.refs_5_
  35.4 1.9 %middle.3 = (bf16[112,340]{1,0:T(8,128)(2,1)S(1)}, bf16[112,340]{1,0:T(8,128)(2,1)S(1)}, bf16[112,128]{1,0:T(8,128)(2,1)S(1)}, bf16[6,112,340]{2,1,0:T(8,128)(2,1)S(1)}, bf16[112,2048]{1,0:T(8,128)(2,1)S(1)}) custom-call(s32[6]{0:T(128)S(1)} %bitcast.21, bf16[6,340,340]{2,1,0:T(8,128)(2,1)S(1)} %get-tuple-element.36.weights, ...), custom_call_target="tpu_custom_call" | custom-call | flops 507687936 | tf_op jit(solution)/shard_map/middle/pallas_call | solution.py:265
  37.3 3.3 %collective-permute-start.12 = (bf16[112,340]{1,0:T(8,128)(2,1)S(1)}, bf16[112,340]{1,0:T(8,128)(2,1)S(1)}, u32[]{:S(2)}, u32[]{:S(2)}) collective-permute-start(bf16[112,340]{1,0:T(8,128)(2,1)S(1)} %get-tuple-element.57.refs_9_), channel_id=1, source_target_pairs={{0,224},{32,64},{64,32},{96,128},{128,96},{160,192},{192,160},{224... | collective-permute-start | bytes 228488 | tf_op jit(solution)/shard_map/ppermute | solution.py:35
  40.7 0.4 collective-permute-start.13
  41.0 1.1 %rest.5 = (bf16[112,340]{1,0:T(8,128)(2,1)S(1)}, bf16[112,340]{1,0:T(8,128)(2,1)S(1)}, bf16[112,340]{1,0:T(8,128)(2,1)S(1)}, bf16[112,340]{1,0:T(8,128)(2,1)S(1)}, bf16[112,128]{1,0:T(8,128)(2,1)S(1)}) custom-call(bf16[112,2048]{1,0:T(8,128)(2,1)S(1)} %get-tuple-element.59.state.refs_14_, bf16[2048,2048]{1,0:T(8,128)(2,1)S(1)} %bitcast.15, ...), custom_call_target="tpu_custom_call" | custom-call | flops 587202560 | tf_op jit(solution)/shard_map/rest/pallas_call | solution.py:216
  42.1 0.8 %collective-permute-start.14 = (bf16[112,340]{1,0:T(8,128)(2,1)S(1)}, bf16[112,340]{1,0:T(8,128)(2,1)S(1)}, u32[]{:S(2)}, u32[]{:S(2)}) collective-permute-start(bf16[112,340]{1,0:T(8,128)(2,1)S(1)} %get-tuple-element.61.refs_12_), channel_id=1, source_target_pairs={{0,1},{1,0},{2,3},{3,2},{4,5},{5,4},{6,7},{7,6},{8,9},{9,8},{10,11... | collective-permute-start | bytes 228488 | tf_op jit(solution)/shard_map/ppermute | solution.py:35
  42.9 1.8 %collective-permute-start.15 = (bf16[112,340]{1,0:T(8,128)(2,1)S(1)}, bf16[112,340]{1,0:T(8,128)(2,1)S(1)}, u32[]{:S(2)}, u32[]{:S(2)}) collective-permute-start(bf16[112,340]{1,0:T(8,128)(2,1)S(1)} %get-tuple-element.62.refs_13_), channel_id=1, source_target_pairs={{0,7},{1,2},{2,1},{3,4},{4,3},{5,6},{6,5},{7,0},{8,15},{9,10},{10,... | collective-permute-start | bytes 228488 | tf_op jit(solution)/shard_map/ppermute | solution.py:35
  44.8 2.0 %collective-permute-start.16 = (bf16[112,340]{1,0:T(8,128)(2,1)S(1)}, bf16[112,340]{1,0:T(8,128)(2,1)S(1)}, u32[]{:S(2)}, u32[]{:S(2)}) collective-permute-start(bf16[112,340]{1,0:T(8,128)(2,1)S(1)} %get-tuple-element.63.refs_11_), channel_id=1, source_target_pairs={{0,24},{8,16},{16,8},{24,0},{1,25},{9,17},{17,9},{25,1},{2,26},{10... | collective-permute-start | bytes 228488 | tf_op jit(solution)/shard_map/ppermute | solution.py:35
  46.8 0.0 collective-permute-done.12.refs_0_
  46.8 0.0 collective-permute-start.17
  46.8 2.6 %gradient.1.refs_7_ = f32[6,340,340]{2,1,0:T(8,128)S(1)} custom-call(bf16[6,112,340]{2,1,0:T(8,128)(2,1)S(1)} %get-tuple-element.66.chosen_a, bf16[6,112,340]{2,1,0:T(8,128)(2,1)S(1)} %get-tuple-element.67.chosen_b, bf16[6,340,340]{2,1,0:T(8,128)(2,1)S(1)} %get-tuple-element.38.choosers, bf16[6,336,340]{2,1,0:T(8,128)(2,1)S(1)} %get-tuple-element.39.stored), custom_call_target="tpu_custom_call" | custom-call | flops 621465600 | tf_op jit(solution)/shard_map/gradient/pallas_call | solution.py:286
  49.4 0.0 collective-permute-done.13.refs_1_
  49.4 0.0 collective-permute-done.14.refs_2_
  49.4 0.0 collective-permute-done.15.refs_3_
  49.4 0.0 collective-permute-done.16.refs_4_
  49.5 0.0 collective-permute-done.17.refs_5_
  49.5 4.4 %last.1 = (bf16[112,2048]{1,0:T(8,128)(2,1)}, bf16[6,340,340]{2,1,0:T(8,128)(2,1)}) custom-call(s32[6]{0:T(128)S(1)} %bitcast.22, bf16[6,340,340]{2,1,0:T(8,128)(2,1)S(1)} %get-tuple-element.36.weights, bf16[112,2048]{1,0:T(8,128)(2,1)S(1)} %get-tuple-element.37.state.seed.refs_13_, bf16[6,340,340]{2,1,0:T(8,128)(2,1)S(1)} %get-tuple-element.38.choosers, ...), custom_call_target="tpu_custom_call" | custom-call | flops 466099200 | tf_op jit(solution)/shard_map/last/pallas_call | solution.py:296
  (1 shorter events, 0.0 us)
Async XLA Ops:
  0.6 8.8 %copy-start = (bf16[1,1,1,2048,2048]{4,3,2,1,0:T(8,128)(2,1)S(1)}, bf16[1,1,1,2048,2048]{4,3,2,1,0:T(8,128)(2,1)}, u32[]{:S(2)}) copy-start(bf16[1,1,1,2048,2048]{4,3,2,1,0:T(8,128)(2,1)} %param.7) | copy-start | bytes 25165828
  3.4 15.4 %collective-permute-start = (bf16[112,340]{1,0:T(8,128)(2,1)S(1)}, bf16[112,340]{1,0:T(8,128)(2,1)S(1)}, u32[]{:S(2)}, u32[]{:S(2)}) collective-permute-start(bf16[112,340]{1,0:T(8,128)(2,1)S(1)} %get-tuple-element.40.refs_8_), channel_id=1, source_target_pairs={{0,224},{32,64},{64,32},{96,128},{128,96},{160,192},{192,160},{224... | collective-permute-start | bytes 228488 | tf_op jit(solution)/shard_map/ppermute | solution.py:35
  9.5 11.3 %collective-permute-start.1 = (bf16[112,340]{1,0:T(8,128)(2,1)S(1)}, bf16[112,340]{1,0:T(8,128)(2,1)S(1)}, u32[]{:S(2)}, u32[]{:S(2)}) collective-permute-start(bf16[112,340]{1,0:T(8,128)(2,1)S(1)} %get-tuple-element.41.refs_7_), channel_id=1, source_target_pairs={{0,32},{32,0},{64,96},{96,64},{128,160},{160,128},{192,224},{224,1... | collective-permute-start | bytes 228488 | tf_op jit(solution)/shard_map/ppermute | solution.py:35
  9.5 9.4 %copy-start.4 = (s32[1,1,1,6,340]{4,2,3,1,0:T(1,128)S(1)}, s32[1,1,1,6,340]{4,2,3,1,0:T(1,128)}, u32[]{:S(2)}) copy-start(s32[1,1,1,6,340]{4,2,3,1,0:T(1,128)} %param.11) | copy-start | bytes 24484
  9.5 9.4 %copy-start.1 = (bf16[1,1,1,6,340,340]{5,4,3,2,1,0:T(8,128)(2,1)S(1)}, bf16[1,1,1,6,340,340]{5,4,3,2,1,0:T(8,128)(2,1)}, u32[]{:S(2)}) copy-start(bf16[1,1,1,6,340,340]{5,4,3,2,1,0:T(8,128)(2,1)} %param.8) | copy-start | bytes 4161604
  9.5 9.4 %copy-start.2 = (bf16[1,1,1,3,112,2048]{5,4,3,2,1,0:T(8,128)(2,1)S(1)}, bf16[1,1,1,3,112,2048]{5,4,3,2,1,0:T(8,128)(2,1)}, u32[]{:S(2)}) copy-start(bf16[1,1,1,3,112,2048]{5,4,3,2,1,0:T(8,128)(2,1)} %param.9) | copy-start | bytes 4128772
  9.5 9.4 %copy-start.3 = (s32[1,1,1,6]{3,2,1,0:T(1,128)S(1)}, s32[1,1,1,6]{3,2,1,0:T(1,128)}, u32[]{:S(2)}) copy-start(s32[1,1,1,6]{3,2,1,0:T(1,128)} %param.10) | copy-start | bytes 76
  10.7 10.1 %collective-permute-start.2 = (bf16[112,340]{1,0:T(8,128)(2,1)S(1)}, bf16[112,340]{1,0:T(8,128)(2,1)S(1)}, u32[]{:S(2)}, u32[]{:S(2)}) collective-permute-start(bf16[112,340]{1,0:T(8,128)(2,1)S(1)} %get-tuple-element.43.refs_11_), channel_id=1, source_target_pairs={{0,1},{1,0},{2,3},{3,2},{4,5},{5,4},{6,7},{7,6},{8,9},{9,8},{10,11... | collective-permute-start | bytes 228488 | tf_op jit(solution)/shard_map/ppermute | solution.py:35
  12.4 8.4 %collective-permute-start.3 = (bf16[112,340]{1,0:T(8,128)(2,1)S(1)}, bf16[112,340]{1,0:T(8,128)(2,1)S(1)}, u32[]{:S(2)}, u32[]{:S(2)}) collective-permute-start(bf16[112,340]{1,0:T(8,128)(2,1)S(1)} %get-tuple-element.44.refs_12_), channel_id=1, source_target_pairs={{0,7},{1,2},{2,1},{3,4},{4,3},{5,6},{6,5},{7,0},{8,15},{9,10},{10,... | collective-permute-start | bytes 228488 | tf_op jit(solution)/shard_map/ppermute | solution.py:35
  17.1 4.4 %collective-permute-start.4 = (bf16[112,340]{1,0:T(8,128)(2,1)S(1)}, bf16[112,340]{1,0:T(8,128)(2,1)S(1)}, u32[]{:S(2)}, u32[]{:S(2)}) collective-permute-start(bf16[112,340]{1,0:T(8,128)(2,1)S(1)} %get-tuple-element.45.refs_10_), channel_id=1, source_target_pairs={{0,24},{8,16},{16,8},{24,0},{1,25},{9,17},{17,9},{25,1},{2,26},{10... | collective-permute-start | bytes 228488 | tf_op jit(solution)/shard_map/ppermute | solution.py:35
  18.9 2.6 %collective-permute-start.5 = (bf16[112,340]{1,0:T(8,128)(2,1)S(1)}, bf16[112,340]{1,0:T(8,128)(2,1)S(1)}, u32[]{:S(2)}, u32[]{:S(2)}) collective-permute-start(bf16[112,340]{1,0:T(8,128)(2,1)S(1)} %get-tuple-element.46.refs_9_), channel_id=1, source_target_pairs={{0,8},{8,0},{16,24},{24,16},{1,9},{9,1},{17,25},{25,17},{2,10},{10... | collective-permute-start | bytes 228488 | tf_op jit(solution)/shard_map/ppermute | solution.py:35
  23.5 9.0 %collective-permute-start.6 = (bf16[112,340]{1,0:T(8,128)(2,1)S(1)}, bf16[112,340]{1,0:T(8,128)(2,1)S(1)}, u32[]{:S(2)}, u32[]{:S(2)}) collective-permute-start(bf16[112,340]{1,0:T(8,128)(2,1)S(1)} %get-tuple-element.48.refs_8_), channel_id=1, source_target_pairs={{0,224},{32,64},{64,32},{96,128},{128,96},{160,192},{192,160},{224... | collective-permute-start | bytes 228488 | tf_op jit(solution)/shard_map/ppermute | solution.py:35
  28.2 4.8 %collective-permute-start.7 = (bf16[112,340]{1,0:T(8,128)(2,1)S(1)}, bf16[112,340]{1,0:T(8,128)(2,1)S(1)}, u32[]{:S(2)}, u32[]{:S(2)}) collective-permute-start(bf16[112,340]{1,0:T(8,128)(2,1)S(1)} %get-tuple-element.49.refs_7_), channel_id=1, source_target_pairs={{0,32},{32,0},{64,96},{96,64},{128,160},{160,128},{192,224},{224,1... | collective-permute-start | bytes 228488 | tf_op jit(solution)/shard_map/ppermute | solution.py:35
  29.4 3.7 %collective-permute-start.8 = (bf16[112,340]{1,0:T(8,128)(2,1)S(1)}, bf16[112,340]{1,0:T(8,128)(2,1)S(1)}, u32[]{:S(2)}, u32[]{:S(2)}) collective-permute-start(bf16[112,340]{1,0:T(8,128)(2,1)S(1)} %get-tuple-element.52.refs_11_), channel_id=1, source_target_pairs={{0,1},{1,0},{2,3},{3,2},{4,5},{5,4},{6,7},{7,6},{8,9},{9,8},{10,11... | collective-permute-start | bytes 228488 | tf_op jit(solution)/shard_map/ppermute | solution.py:35
  29.5 4.9 %collective-permute-start.9 = (bf16[112,340]{1,0:T(8,128)(2,1)S(1)}, bf16[112,340]{1,0:T(8,128)(2,1)S(1)}, u32[]{:S(2)}, u32[]{:S(2)}) collective-permute-start(bf16[112,340]{1,0:T(8,128)(2,1)S(1)} %get-tuple-element.53.refs_12_), channel_id=1, source_target_pairs={{0,7},{1,2},{2,1},{3,4},{4,3},{5,6},{6,5},{7,0},{8,15},{9,10},{10,... | collective-permute-start | bytes 228488 | tf_op jit(solution)/shard_map/ppermute | solution.py:35
  30.9 4.5 %collective-permute-start.10 = (bf16[112,340]{1,0:T(8,128)(2,1)S(1)}, bf16[112,340]{1,0:T(8,128)(2,1)S(1)}, u32[]{:S(2)}, u32[]{:S(2)}) collective-permute-start(bf16[112,340]{1,0:T(8,128)(2,1)S(1)} %get-tuple-element.54.refs_10_), channel_id=1, source_target_pairs={{0,24},{8,16},{16,8},{24,0},{1,25},{9,17},{17,9},{25,1},{2,26},{10... | collective-permute-start | bytes 228488 | tf_op jit(solution)/shard_map/ppermute | solution.py:35
  32.5 2.9 %collective-permute-start.11 = (bf16[112,340]{1,0:T(8,128)(2,1)S(1)}, bf16[112,340]{1,0:T(8,128)(2,1)S(1)}, u32[]{:S(2)}, u32[]{:S(2)}) collective-permute-start(bf16[112,340]{1,0:T(8,128)(2,1)S(1)} %get-tuple-element.55.refs_9_), channel_id=1, source_target_pairs={{0,8},{8,0},{16,24},{24,16},{1,9},{9,1},{17,25},{25,17},{2,10},{10... | collective-permute-start | bytes 228488 | tf_op jit(solution)/shard_map/ppermute | solution.py:35
  37.3 9.5 %collective-permute-start.12 = (bf16[112,340]{1,0:T(8,128)(2,1)S(1)}, bf16[112,340]{1,0:T(8,128)(2,1)S(1)}, u32[]{:S(2)}, u32[]{:S(2)}) collective-permute-start(bf16[112,340]{1,0:T(8,128)(2,1)S(1)} %get-tuple-element.57.refs_9_), channel_id=1, source_target_pairs={{0,224},{32,64},{64,32},{96,128},{128,96},{160,192},{192,160},{224... | collective-permute-start | bytes 228488 | tf_op jit(solution)/shard_map/ppermute | solution.py:35
  40.7 8.8 %collective-permute-start.13 = (bf16[112,340]{1,0:T(8,128)(2,1)S(1)}, bf16[112,340]{1,0:T(8,128)(2,1)S(1)}, u32[]{:S(2)}, u32[]{:S(2)}) collective-permute-start(bf16[112,340]{1,0:T(8,128)(2,1)S(1)} %get-tuple-element.58.refs_8_), channel_id=1, source_target_pairs={{0,32},{32,0},{64,96},{96,64},{128,160},{160,128},{192,224},{224,1... | collective-permute-start | bytes 228488 | tf_op jit(solution)/shard_map/ppermute | solution.py:35
  42.1 7.3 %collective-permute-start.14 = (bf16[112,340]{1,0:T(8,128)(2,1)S(1)}, bf16[112,340]{1,0:T(8,128)(2,1)S(1)}, u32[]{:S(2)}, u32[]{:S(2)}) collective-permute-start(bf16[112,340]{1,0:T(8,128)(2,1)S(1)} %get-tuple-element.61.refs_12_), channel_id=1, source_target_pairs={{0,1},{1,0},{2,3},{3,2},{4,5},{5,4},{6,7},{7,6},{8,9},{9,8},{10,11... | collective-permute-start | bytes 228488 | tf_op jit(solution)/shard_map/ppermute | solution.py:35
  42.9 6.5 %collective-permute-start.15 = (bf16[112,340]{1,0:T(8,128)(2,1)S(1)}, bf16[112,340]{1,0:T(8,128)(2,1)S(1)}, u32[]{:S(2)}, u32[]{:S(2)}) collective-permute-start(bf16[112,340]{1,0:T(8,128)(2,1)S(1)} %get-tuple-element.62.refs_13_), channel_id=1, source_target_pairs={{0,7},{1,2},{2,1},{3,4},{4,3},{5,6},{6,5},{7,0},{8,15},{9,10},{10,... | collective-permute-start | bytes 228488 | tf_op jit(solution)/shard_map/ppermute | solution.py:35
  44.8 4.7 %collective-permute-start.16 = (bf16[112,340]{1,0:T(8,128)(2,1)S(1)}, bf16[112,340]{1,0:T(8,128)(2,1)S(1)}, u32[]{:S(2)}, u32[]{:S(2)}) collective-permute-start(bf16[112,340]{1,0:T(8,128)(2,1)S(1)} %get-tuple-element.63.refs_11_), channel_id=1, source_target_pairs={{0,24},{8,16},{16,8},{24,0},{1,25},{9,17},{17,9},{25,1},{2,26},{10... | collective-permute-start | bytes 228488 | tf_op jit(solution)/shard_map/ppermute | solution.py:35
  46.8 2.7 %collective-permute-start.17 = (bf16[112,340]{1,0:T(8,128)(2,1)S(1)}, bf16[112,340]{1,0:T(8,128)(2,1)S(1)}, u32[]{:S(2)}, u32[]{:S(2)}) collective-permute-start(bf16[112,340]{1,0:T(8,128)(2,1)S(1)} %get-tuple-element.64.refs_10_), channel_id=1, source_target_pairs={{0,8},{8,0},{16,24},{24,16},{1,9},{9,1},{17,25},{25,17},{2,10},{10... | collective-permute-start | bytes 228488 | tf_op jit(solution)/shard_map/ppermute | solution.py:35
